TPU v7x, 256 devices: a whole 4x4x8 slice. The times are simulated.
256 devices in a mesh: expert: 8 (over x_lo, y), dp: 32 (over z, x_hi, core).
Axes of the slice: x: 4 (x_hi: 2, x_lo: 2; x = x_hi * 2 + x_lo), y: 4, z: 8, core: 2. Of those that a mesh axis runs over, the one named last changes fastest.
Arguments:
- activations: bfloat16 [4096, 3584], P('dp'), may hold values from -6 to 6
- cotangent: bfloat16 [4096, 3584], P('dp'), may hold values from -6 to 6
- expert_ids: int32 [32, 2], P('dp'), may hold values from 0 to 7, all different within a row
- slot_rows: int32 [32, 2, 128], P('dp'), may hold values from 0 to 127, as said below
- slot_counts: int32 [32, 2], P('dp'), may hold values from 32 to 128, as said below
- route_probs: float32 [32, 2, 128], P('dp'), may hold values from 0.05 to 1
- w_gate: bfloat16 [8, 3584, 2432], P(None, 'dp', 'expert'), may hold values from -0.09375 to 0.09375
- w_up: bfloat16 [8, 3584, 2432], P(None, 'dp', 'expert'), may hold values from -0.09375 to 0.09375
- w_down: bfloat16 [8, 2432, 3584], P(None, 'expert', 'dp'), may hold values from -0.125 to 0.125
Outputs:
- grad_activations: float32 [4096, 3584], P('dp', 'expert')
- grad_gate: float32 [8, 3584, 2432], P(None, 'dp', 'expert')
- grad_up: float32 [8, 3584, 2432], P(None, 'dp', 'expert')
- grad_down: float32 [8, 2432, 3584], P(None, 'expert', 'dp')
Inputs may be any that keep to these rules, and one draw needn't show every extreme that they name: `slot_rows`: each group's list for one slot is a permutation of the 128 row indices of that group. `slot_counts`: some slot of some group uses all 128 rows. `expert_ids`: the 2 ids of one group are distinct, and every expert is named by some group.
All inputs are finite; a program needn't handle non-finite values.
Results may differ from a plain program's by a relative error of at most 0.005.
Values may be sent and summed in bfloat16 or wider, within the bound.
A program may use at most 128 MiB of HBM per device.

v0:
```python
import jax
import jax.numpy as jnp
from jax import lax
from jax.sharding import PartitionSpec as P


def shards(
    activations, cotangent, expert_ids, slot_rows, slot_counts, route_probs, w_gate, w_up, w_down
):
    ids = expert_ids[0]
    rows = slot_rows[0]
    counts = slot_counts[0]
    probs = route_probs[0]
    slots = ids.shape[0]
    groups = lax.axis_size("dp")
    block = w_gate.shape[1]
    width = w_gate.shape[2]
    experts = w_gate.shape[0]
    tok_rows = activations.shape[0]
    model_width = activations.shape[1]
    all_ids = lax.all_gather(ids[None, :], "dp", axis=0, tiled=True)
    order = all_ids.T
    pulled_gate, pulled_up, pulled_down = (
        lax.all_to_all(w_gate[order], "dp", split_axis=1, concat_axis=1, tiled=True),
        lax.all_to_all(w_up[order], "dp", split_axis=1, concat_axis=1, tiled=True),
        lax.all_to_all(w_down[order], "dp", split_axis=1, concat_axis=1, tiled=True),
    )
    position = jnp.arange(tok_rows, dtype=jnp.int32)
    expert_iota = jnp.arange(experts, dtype=jnp.int32)
    xs_split = activations.reshape(tok_rows, groups, block)
    grad_rows = jnp.zeros((tok_rows, model_width), jnp.float32)
    gate_parts = []
    up_parts = []
    down_parts = []
    for slot in range(slots):
        wg = pulled_gate[slot].reshape(groups * block, width)
        wu = pulled_up[slot].reshape(groups * block, width)
        wd = pulled_down[slot]
        picked = rows[slot]
        scale = jnp.where(position < counts[slot], probs[slot], jnp.float32(0.0))
        row_scale = jnp.zeros((tok_rows,), jnp.float32).at[picked].set(scale)
        dys = (cotangent.astype(jnp.float32) * row_scale[:, None]).astype(jnp.bfloat16)
        dys_split = dys.reshape(tok_rows, groups, block)
        gval = jnp.dot(activations, wg, preferred_element_type=jnp.float32)
        uval = jnp.dot(activations, wu, preferred_element_type=jnp.float32)
        sig = jax.nn.sigmoid(gval)
        act = gval * sig
        hidden = (act * uval).astype(jnp.bfloat16)
        dhid = jnp.einsum("cnb,nfb->cf", dys_split, wd, preferred_element_type=jnp.float32)
        dgate = (dhid * uval * sig * (1.0 + gval * (1.0 - sig))).astype(jnp.bfloat16)
        dup = (dhid * act).astype(jnp.bfloat16)
        part_gate = jnp.einsum(
            "cnb,cf->nbf", xs_split, dgate, preferred_element_type=jnp.float32
        ).astype(jnp.bfloat16)
        part_up = jnp.einsum(
            "cnb,cf->nbf", xs_split, dup, preferred_element_type=jnp.float32
        ).astype(jnp.bfloat16)
        part_down = jnp.einsum(
            "cf,cnb->nfb", hidden, dys_split, preferred_element_type=jnp.float32
        ).astype(jnp.bfloat16)
        term = jnp.einsum("cf,df->cd", dgate, wg, preferred_element_type=jnp.float32)
        term = term + jnp.einsum("cf,df->cd", dup, wu, preferred_element_type=jnp.float32)
        grad_rows = grad_rows + term
        gate_parts.append(part_gate)
        up_parts.append(part_up)
        down_parts.append(part_down)
    back_gate, back_up, back_down = (
        lax.all_to_all(
            jnp.stack(gate_parts, axis=0), "dp", split_axis=1, concat_axis=1, tiled=True
        ),
        lax.all_to_all(jnp.stack(up_parts, axis=0), "dp", split_axis=1, concat_axis=1, tiled=True),
        lax.all_to_all(
            jnp.stack(down_parts, axis=0), "dp", split_axis=1, concat_axis=1, tiled=True
        ),
    )
    owners = (all_ids.T[None, :, :] == expert_iota[:, None, None]).astype(jnp.bfloat16)
    grad_gate = jnp.einsum("esn,snbf->ebf", owners, back_gate, preferred_element_type=jnp.float32)
    grad_up = jnp.einsum("esn,snbf->ebf", owners, back_up, preferred_element_type=jnp.float32)
    grad_down = jnp.einsum("esn,snfb->efb", owners, back_down, preferred_element_type=jnp.float32)
    grad_activations = lax.psum_scatter(grad_rows, "expert", scatter_dimension=1, tiled=True)
    return (grad_activations, grad_gate, grad_up, grad_down)


def solution(mesh):
    return jax.shard_map(
        shards,
        mesh=mesh,
        in_specs=(
            P("dp", None),
            P("dp", None),
            P("dp", None),
            P("dp", None, None),
            P("dp", None),
            P("dp", None, None),
            P(None, "dp", "expert"),
            P(None, "dp", "expert"),
            P(None, "expert", "dp"),
        ),
        out_specs=(
            P("dp", "expert"),
            P(None, "dp", "expert"),
            P(None, "dp", "expert"),
            P(None, "expert", "dp"),
        ),
        check_vma=False,
    )
```

profile of v0, /device:TPU:72, one launch (start us, length us, event | category | flops | bytes accessed | tf_op | source)
XLA Modules:
  0.0 793.9 jit_solution(13110555424070084443)
XLA Ops:
  7.2 39.7 %all-gather = s32[32,1,2]{2,1,0:T(1,128)S(1)} all-gather(s32[1,1,2]{2,1,0:T(1,128)} %bitcast.165), channel_id=1, replica_groups=mesh['expert'=8,'dp'=32] {'dp'}, dimensions={0}, use_global_device_ids=true | all-gather | bytes 264 | tf_op jit(solution)/shard_map/all_gather | solution.py:21
  47.0 3.5 gather_fusion.2
  50.5 5.0 copy.63
  55.5 9.4 %all-to-all-start.2 = ((bf16[2,32,112,304]{2,3,0,1:T(8,128)(2,1)}), bf16[2,32,112,304]{2,3,0,1:T(8,128)(2,1)}, u32[]{:S(2)}, u32[]{:S(2)}) async-start(bf16[2,32,112,304]{2,3,0,1:T(8,128)(2,1)} %copy.63), calls=%async_computation.2 | async-start | bytes 9961472 | tf_op jit(solution)/shard_map/all_to_all | solution.py:24
  65.0 3.4 gather_fusion.1
  68.4 5.0 copy.61
  73.4 103.2 %all-to-all-done.2 = bf16[2,32,112,304]{2,3,0,1:T(8,128)(2,1)} async-done(((bf16[2,32,112,304]{2,3,0,1:T(8,128)(2,1)}), bf16[2,32,112,304]{2,3,0,1:T(8,128)(2,1)}, u32[]{:S(2)}, u32[]{:S(2)}) %all-to-all-start.2) | async-done | bytes 4358176 | tf_op jit(solution)/shard_map/all_to_all | solution.py:24
  176.6 7.0 all-to-all-start.1
  183.6 3.4 gather_fusion
  187.0 5.0 copy.59
  192.0 103.1 %all-to-all-done.1 = bf16[2,32,112,304]{2,3,0,1:T(8,128)(2,1)} async-done(((bf16[2,32,112,304]{2,3,0,1:T(8,128)(2,1)}), bf16[2,32,112,304]{2,3,0,1:T(8,128)(2,1)}, u32[]{:S(2)}, u32[]{:S(2)}) %all-to-all-start.1) | async-done | bytes 4358176 | tf_op jit(solution)/shard_map/all_to_all | solution.py:25
  295.1 6.9 all-to-all-start
  302.7 1.3 copy.68
  304.6 1.3 compare_select_fusion.3
  308.0 1.5 fusion.10
  309.6 4.2 fusion.50
  313.8 2.1 copy.64
  315.9 5.1 reshape_squeeze.13
  321.0 4.3 fusion.49
  325.3 2.1 copy.62
  327.4 6.0 reshape_squeeze.12
  333.4 3.8 copy.67
  337.1 6.0 reshape_squeeze.15
  343.1 3.8 copy.66
  346.9 6.2 reshape_squeeze.14
  356.3 1.4 convolution_bitcast_fusion
  357.9 1.4 convolution_bitcast_fusion.1
  359.3 54.3 %all-to-all-done = bf16[2,32,304,112]{3,2,0,1:T(8,128)(2,1)} async-done(((bf16[2,32,304,112]{3,2,0,1:T(8,128)(2,1)}), bf16[2,32,304,112]{3,2,0,1:T(8,128)(2,1)}, u32[]{:S(2)}, u32[]{:S(2)}) %all-to-all-start) | async-done | bytes 4358176 | tf_op jit(solution)/shard_map/all_to_all | solution.py:26
  413.6 3.5 multiply_convert_fusion.2
  418.2 3.1 multiply_convert_fusion.4
  423.3 2.6 copy.71
  426.0 6.9 all-to-all-start.4
  432.9 1.8 convert_bitcast_fusion.4
  436.7 2.5 copy.69
  439.2 105.2 %all-to-all-done.4 = bf16[2,32,112,304]{2,3,0,1:T(8,128)(2,1)} async-done(((bf16[2,32,112,304]{2,3,0,1:T(8,128)(2,1)}), bf16[2,32,112,304]{2,3,0,1:T(8,128)(2,1)}, u32[]{:S(2)}, u32[]{:S(2)}) %all-to-all-start.4) | async-done | bytes 4358176 | tf_op jit(solution)/shard_map/all_to_all | solution.py:71
  544.4 6.9 all-to-all-start.3
  551.4 1.9 convert_bitcast_fusion
  555.3 2.6 copy.73
  558.0 105.0 %all-to-all-done.3 = bf16[2,32,112,304]{2,3,0,1:T(8,128)(2,1)} async-done(((bf16[2,32,112,304]{2,3,0,1:T(8,128)(2,1)}), bf16[2,32,112,304]{2,3,0,1:T(8,128)(2,1)}, u32[]{:S(2)}, u32[]{:S(2)}) %all-to-all-start.3) | async-done | bytes 4358176 | tf_op jit(solution)/shard_map/all_to_all | solution.py:68
  662.9 6.9 all-to-all-start.5
  675.0 2.5 fusion.6
  677.6 3.9 fusion.14
  681.5 1.3 copy.76
  682.7 3.9 fusion.11
  686.6 1.3 copy.75
  687.8 93.5 %all-to-all-done.5 = bf16[2,32,304,112]{3,2,0,1:T(8,128)(2,1)} async-done(((bf16[2,32,304,112]{3,2,0,1:T(8,128)(2,1)}), bf16[2,32,304,112]{3,2,0,1:T(8,128)(2,1)}, u32[]{:S(2)}, u32[]{:S(2)}) %all-to-all-start.5) | async-done | bytes 4358176 | tf_op jit(solution)/shard_map/all_to_all | solution.py:72
  781.4 3.9 fusion.17
  785.3 1.3 copy.77
  (72 shorter events, 19.2 us)
Async XLA Ops:
  7.2 39.9 %copy-start = (bf16[8,112,304]{1,2,0:T(8,128)(2,1)S(1)}, bf16[8,112,304]{1,2,0:T(8,128)(2,1)}, u32[]{:S(2)}) copy-start(bf16[8,112,304]{1,2,0:T(8,128)(2,1)} %param.15) | copy-start | bytes 1634308
  55.5 9.4 %copy-start.2 = (bf16[8,112,304]{1,2,0:T(8,128)(2,1)S(1)}, bf16[8,112,304]{1,2,0:T(8,128)(2,1)}, u32[]{:S(2)}) copy-start(bf16[8,112,304]{1,2,0:T(8,128)(2,1)} %param.16) | copy-start | bytes 1634308
  55.5 121.1 %all-to-all-start.2 = ((bf16[2,32,112,304]{2,3,0,1:T(8,128)(2,1)}), bf16[2,32,112,304]{2,3,0,1:T(8,128)(2,1)}, u32[]{:S(2)}, u32[]{:S(2)}) async-start(bf16[2,32,112,304]{2,3,0,1:T(8,128)(2,1)} %copy.63), calls=%async_computation.2 | async-start | bytes 9961472 | tf_op jit(solution)/shard_map/all_to_all | solution.py:24
  176.6 7.0 copy-start.3
  176.6 118.5 %all-to-all-start.1 = ((bf16[2,32,112,304]{2,3,0,1:T(8,128)(2,1)}), bf16[2,32,112,304]{2,3,0,1:T(8,128)(2,1)}, u32[]{:S(2)}, u32[]{:S(2)}) async-start(bf16[2,32,112,304]{2,3,0,1:T(8,128)(2,1)} %copy.61), calls=%async_computation.1 | async-start | bytes 9961472 | tf_op jit(solution)/shard_map/all_to_all | solution.py:25
  192.0 110.0 %copy-start.15 = (bf16[128,3584]{1,0:T(8,128)(2,1)S(1)}, bf16[128,3584]{1,0:T(8,128)(2,1)}, u32[]{:S(2)}) copy-start(bf16[128,3584]{1,0:T(8,128)(2,1)} %param.10) | copy-start | bytes 2752516
  192.0 110.7 %copy-start.10 = (bf16[128,3584]{1,0:T(8,128)(2,1)S(1)}, bf16[128,3584]{1,0:T(8,128)(2,1)}, u32[]{:S(2)}) copy-start(bf16[128,3584]{1,0:T(8,128)(2,1)} %param.9) | copy-start | bytes 2752516
  295.1 118.4 %all-to-all-start = ((bf16[2,32,304,112]{3,2,0,1:T(8,128)(2,1)}), bf16[2,32,304,112]{3,2,0,1:T(8,128)(2,1)}, u32[]{:S(2)}, u32[]{:S(2)}) async-start(bf16[2,32,304,112]{3,2,0,1:T(8,128)(2,1)} %copy.59), calls=%async_computation | async-start | bytes 9961472 | tf_op jit(solution)/shard_map/all_to_all | solution.py:26
  302.0 1.9 copy-start.21
  302.0 2.5 copy-start.23
  302.1 2.5 copy-start.22
  353.1 1.6 copy-start.4
  354.7 1.6 copy-start.6
  356.3 1.6 copy-start.8
  413.6 3.5 copy-start.11
  417.0 1.2 copy-start.12
  421.4 2.0 copy-start.17
  426.0 118.5 %all-to-all-start.4 = ((bf16[2,32,112,304]{2,3,0,1:T(8,128)(2,1)}), bf16[2,32,112,304]{2,3,0,1:T(8,128)(2,1)}, u32[]{:S(2)}, u32[]{:S(2)}) async-start(bf16[2,32,112,304]{2,3,0,1:T(8,128)(2,1)} %copy.71), calls=%async_computation.5 | async-start | bytes 9961472 | tf_op jit(solution)/shard_map/all_to_all | solution.py:71
  432.9 1.8 copy-start.19
  439.2 112.2 %copy-start.14 = (bf16[128,3584]{0,1:T(8,128)(2,1)S(1)}, bf16[128,3584]{0,1:T(8,128)(2,1)}, u32[]{:S(2)}) copy-start(bf16[128,3584]{0,1:T(8,128)(2,1)} %get-tuple-element.24) | copy-start | bytes 2752516
  544.4 118.5 %all-to-all-start.3 = ((bf16[2,32,112,304]{2,3,0,1:T(8,128)(2,1)}), bf16[2,32,112,304]{2,3,0,1:T(8,128)(2,1)}, u32[]{:S(2)}, u32[]{:S(2)}) async-start(bf16[2,32,112,304]{2,3,0,1:T(8,128)(2,1)} %copy.69), calls=%async_computation.4 | async-start | bytes 9961472 | tf_op jit(solution)/shard_map/all_to_all | solution.py:68
  551.4 1.9 copy-start.13
  557.9 112.2 %copy-start.20 = (bf16[128,304]{0,1:T(8,128)(2,1)S(1)}, bf16[128,304]{0,1:T(8,128)(2,1)}, u32[]{:S(2)}) copy-start(bf16[128,304]{0,1:T(8,128)(2,1)} %get-tuple-element.29) | copy-start | bytes 233476
  662.9 118.5 %all-to-all-start.5 = ((bf16[2,32,304,112]{3,2,0,1:T(8,128)(2,1)}), bf16[2,32,304,112]{3,2,0,1:T(8,128)(2,1)}, u32[]{:S(2)}, u32[]{:S(2)}) async-start(bf16[2,32,304,112]{3,2,0,1:T(8,128)(2,1)} %copy.73), calls=%async_computation.6 | async-start | bytes 9961472 | tf_op jit(solution)/shard_map/all_to_all | solution.py:72
  669.8 1.5 copy-start.16
  669.9 116.7 %reduce-scatter.2.cloned.1.call-start = ((), (), s32[]{:S(2)}) async-start(), calls=%async_computation.7 | async-start | bytes 2064384 | tf_op jit(solution)/shard_map/reduce_scatter | solution.py:80
  670.2 1.6 copy-start.7
  671.8 1.6 copy-start.5
  671.8 1.6 copy-start.18
  673.4 1.6 copy-start.9
  781.4 5.2 copy-start.1
Sparse Core Ops, SparseCore 0:
  677.7 51.9 reduce-scatter.1
where the time goes:
time: 803 us; the launch traced here: 794 us
  waiting for transfers between devices  564 us (70%)
  local copies, waits for them, and re-layouts  88.8 us (11%)
  starting transfers between devices  44.3 us (6%)
  blocking collectives  39.7 us (5%)
  matrix products  35.6 us (4%)
  between operations  14.9 us (2%)
    all_to_all x1, waiting for transfers between devices, shards(): lax.all_to_all(jnp.stack(up_parts, axis=0), 'dp', split_axis=1, concat_ax...  105 us
    all_to_all x1, waiting for transfers between devices, shards(): lax.all_to_all(jnp.stack(gate_parts, axis=0), 'dp', split_axis=1, concat_...  105 us
    all_to_all x1, waiting for transfers between devices, shards(): lax.all_to_all(w_gate[order], 'dp', split_axis=1, concat_axis=1, tiled=True)  103 us
    all_to_all x1, waiting for transfers between devices, shards(): lax.all_to_all(w_up[order], 'dp', split_axis=1, concat_axis=1, tiled=True)  103 us
    all_to_all x1, waiting for transfers between devices, shards(): lax.all_to_all(jnp.stack(down_parts, axis=0), 'dp', split_axis=1, concat_...  93.5 us
    all_to_all x1, waiting for transfers between devices, shards(): lax.all_to_all(w_down[order], 'dp', split_axis=1, concat_axis=1, tiled=True)  54.3 us
    all_gather x1, blocking collectives, shards(): all_ids = lax.all_gather(ids[None, :], 'dp', axis=0, tiled=True)  39.7 us
  transfers between devices with their start and end apart: 7, of which 6 were waited for; matrix products, arithmetic and copies ran while one was open for 13% of the time, Pallas kernels for 0%

commit v1 on v0

v1 whole, which is shorter than its diff:
```python
import functools

import jax
import jax.numpy as jnp
from jax import lax
from jax.experimental import pallas as pl
from jax.experimental.pallas import tpu as pltpu
from jax.sharding import PartitionSpec as P

MESH = pl.DeviceIdType.MESH
F32 = jnp.float32
BF16 = jnp.bfloat16

NZ, NXH, NC, NXL, NY = 8, 2, 2, 2, 4
SLOTS = 2
EXPERTS = 8
TOK = 128
SUB = 112
DZ = 448
FH = 152
F3 = 3 * FH
FP = 464
VMEM_LIMIT = 58 * 1024 * 1024


def place():
    ex = lax.axis_index("expert")
    dp = lax.axis_index("dp")
    return ex // NY, ex % NY, dp // 4, (dp // 2) % 2, dp % 2


def device(xl, y, z, xh, c):
    return (xl * NY + y, z * 4 + xh * 2 + c)


def remote(src, dst, ssem, rsem, dev):
    return pltpu.make_async_remote_copy(
        src_ref=src, dst_ref=dst, send_sem=ssem, recv_sem=rsem, device_id=dev, device_id_type=MESH
    )


def greet(devices):
    barrier = pltpu.get_barrier_semaphore()
    for dev in devices:
        pl.semaphore_signal(barrier, inc=1, device_id=dev, device_id_type=MESH)
    pl.semaphore_wait(barrier, len(devices))


def x_peers(xl, y, z, xh, c):
    pos = xh * 2 + xl
    out = []
    for step in range(1, 4):
        to = (pos + step) % 4
        out.append(device(to % 2, y, z, to // 2, c))
    return out


def y_peers(xl, y, z, xh, c):
    return [device(xl, (y + step) % NY, z, xh, c) for step in range(1, NY)]


def z_peers(xl, y, z, xh, c):
    return [device(xl, y, (z + step) % NZ, xh, c) for step in range(1, NZ)]


def exchange_kernel(
    piece, info, wsend, x_out, info_out, w_out,
    zs, zr, is_, ir, xs, xr, ixs, ixr, ys, yr, ws, wr, loc,
):
    xl, y, z, xh, c = me = place()
    zp, xp, yp = z_peers(*me), x_peers(*me), y_peers(*me)
    far = device(xl, y, z, 1 - xh, c)
    twin = device(xl, y, z, xh, 1 - c)
    greet(zp + xp + yp + [twin])

    cz = []
    for i in range(NZ - 1):
        to = (z + i + 1) % NZ
        cz.append(remote(piece.at[to], x_out.at[xh, xl, y, z], zs.at[i], zr.at[i], zp[i]))
        cz[-1].start()
    ci = []
    for i in range(NZ - 1):
        ci.append(remote(info, info_out.at[xh, z], is_.at[i], ir.at[i], zp[i]))
        ci[-1].start()
    wfar = remote(wsend.at[1 - xh], w_out.at[xh, c], ws.at[0], wr.at[0], far)
    wfar.start()
    wown = remote(wsend.at[xh], w_out.at[xh, c], ws.at[1], wr.at[1], twin)
    wown.start()
    here = [
        pltpu.make_async_copy(piece.at[z], x_out.at[xh, xl, y, z], loc.at[0]),
        pltpu.make_async_copy(info, info_out.at[xh, z], loc.at[1]),
        pltpu.make_async_copy(wsend.at[xh], w_out.at[xh, c], loc.at[2]),
    ]
    for h in here:
        h.start()
    for h in here:
        h.wait()
    for k in cz:
        k.wait()
    cx = []
    for i in range(3):
        cx.append(remote(x_out.at[xh, xl, y], x_out.at[xh, xl, y], xs.at[i], xr.at[i], xp[i]))
        cx[-1].start()
    for k in ci:
        k.wait()
    cinf = remote(info_out.at[xh], info_out.at[xh], ixs.at[0], ixr.at[0], far)
    cinf.start()
    for k in cx:
        k.wait()
    cy = []
    for i in range(3):
        cy.append(remote(x_out.at[:, :, y], x_out.at[:, :, y], ys.at[i], yr.at[i], yp[i]))
        cy[-1].start()
    wfar.wait()
    wpass = remote(w_out.at[1 - xh, c], w_out.at[1 - xh, c], ws.at[2], wr.at[2], twin)
    wpass.start()
    for k in cy:
        k.wait()
    cinf.wait()
    wown.wait()
    wpass.wait()


def exchange(piece, info, wsend):
    dma = pltpu.SemaphoreType.DMA
    anys = pl.BlockSpec(memory_space=pl.ANY)
    return pl.pallas_call(
        exchange_kernel,
        out_shape=(
            jax.ShapeDtypeStruct((NXH, NXL, NY, NZ, SUB, TOK), BF16),
            jax.ShapeDtypeStruct((NXH, NZ, 8, TOK), F32),
            jax.ShapeDtypeStruct((NXH, NC, EXPERTS, SUB, FP), BF16),
        ),
        in_specs=[anys] * 3,
        out_specs=(anys,) * 3,
        scratch_shapes=[dma((7,))] * 4 + [dma((3,))] * 2 + [dma((1,))] * 2 + [dma((3,))] * 2
        + [dma((3,))] * 2 + [dma((3,))],
        compiler_params=pltpu.CompilerParams(collective_id=0, has_side_effects=True),
        name="exchange_in",
    )(piece, info, wsend)


def hidden_kernel(ids, x, w, scale, h, acc, own, rs_s, rs_r, ag_s, ag_r):
    xl, y, z, xh, c = place()
    up = device(xl, y, (z + 1) % NZ, xh, c)
    down = device(xl, y, (z + NZ - 1) % NZ, xh, c)
    greet([up, down])
    to = (up, down)

    def partial(group_z, half, slot):
        e = ids[half * (NZ * SLOTS) + group_z * SLOTS + slot]
        xt = x[half, 0, :, group_z].reshape(DZ, TOK)
        dyt = x[half, 1, :, group_z].reshape(DZ, TOK)
        dys = (dyt.astype(F32) * scale[half, group_z, pl.ds(slot, 1), :]).astype(BF16)
        gu = jnp.dot(w[e, 0 : 2 * FH, :], xt, preferred_element_type=F32)
        dh = jnp.dot(w[e, 2 * FH : FP, :], dys, preferred_element_type=F32)
        return gu, dh[:FH]

    def put(half, slot, gu, dh):
        own[half, slot, 0 : 2 * FH, :] = gu
        own[half, slot, 2 * FH : F3, :] = dh

    def chunk(half, s):
        return (z + NZ - 1 - s) % NZ if half == 0 else (z + 1 + s) % NZ

    def hop(half, slot, s, src):
        return remote(
            src, acc.at[half, s, slot], rs_s.at[half, s, slot], rs_r.at[half, s, slot], to[half]
        )

    for half in range(2):
        for slot in range(SLOTS):
            put(half, slot, *partial(chunk(half, 0), half, slot))
            hop(half, slot, 0, own.at[half, slot]).start()
    for half in range(2):
        for slot in range(SLOTS):
            hop(half, slot, 0, own.at[half, slot]).wait_send()

    def ring(s, carry):
        for half in range(2):
            for slot in range(SLOTS):
                put(half, slot, *partial(chunk(half, s), half, slot))
        for slot in range(SLOTS):
            for half in range(2):
                here = acc.at[half, s - 1, slot]
                hop(half, slot, s - 1, here).wait_recv()
                acc[half, s - 1, slot] = acc[half, s - 1, slot] + own[half, slot]
                hop(half, slot, s, here).start()
        return carry

    lax.fori_loop(1, NZ - 1, ring, 0)

    def gather(half, slot, s, group_z):
        ref = h.at[group_z, half, slot]
        return remote(ref, ref, ag_s.at[half, s, slot], ag_r.at[half, s, slot], to[half])

    def origin(half, s):
        return (z + NZ - s) % NZ if half == 0 else (z + s) % NZ

    for half in range(2):
        for slot in range(SLOTS):
            put(half, slot, *partial(z, half, slot))
    for slot in range(SLOTS):
        for half in range(2):
            last = acc.at[half, NZ - 2, slot]
            hop(half, slot, NZ - 2, last).wait_recv()
            g = acc[half, NZ - 2, slot, 0:FH, :] + own[half, slot, 0:FH, :]
            u = acc[half, NZ - 2, slot, FH : 2 * FH, :] + own[half, slot, FH : 2 * FH, :]
            dh = acc[half, NZ - 2, slot, 2 * FH : F3, :] + own[half, slot, 2 * FH : F3, :]
            sig = 1.0 / (1.0 + jnp.exp(-g))
            act = g * sig
            dg = dh * u * sig * (1.0 + g * (1.0 - sig))
            du = dh * act
            hid = act * u
            h[z, half, slot, 0 : 2 * FH, :] = jnp.concatenate([dg, du], axis=0).astype(BF16)
            h[z, half, slot, 2 * FH : FP, :] = jnp.concatenate(
                [hid, jnp.zeros((FP - F3, TOK), F32)], axis=0
            ).astype(BF16)
            gather(half, slot, 0, z).start()

    def pass_on(s, carry):
        for slot in range(SLOTS):
            for half in range(2):
                gather(half, slot, s - 1, origin(half, s)).wait_recv()
                gather(half, slot, s, origin(half, s)).start()
        return carry

    lax.fori_loop(1, NZ - 1, pass_on, 0)
    for half in range(2):
        for slot in range(SLOTS):
            gather(half, slot, NZ - 2, origin(half, NZ - 1)).wait_recv()

    def drain(s, carry):
        for half in range(2):
            for slot in range(SLOTS):
                hop(half, slot, s, acc.at[half, s - 1, slot]).wait_send()
                gather(half, slot, s, origin(half, s)).wait_send()
        return carry

    lax.fori_loop(1, NZ - 1, drain, 0)
    for half in range(2):
        for slot in range(SLOTS):
            gather(half, slot, 0, z).wait_send()


def hidden_grads(ids, x, w, scale):
    dma = pltpu.SemaphoreType.DMA
    vm = pl.BlockSpec(memory_space=pltpu.VMEM)
    return pl.pallas_call(
        hidden_kernel,
        out_shape=jax.ShapeDtypeStruct((NZ, NXH, SLOTS, FP, TOK), BF16),
        in_specs=[pl.BlockSpec(memory_space=pltpu.SMEM), vm, vm, vm],
        out_specs=vm,
        scratch_shapes=[
            pltpu.VMEM((2, NZ - 1, SLOTS, F3, TOK), F32),
            pltpu.VMEM((2, SLOTS, F3, TOK), F32),
        ]
        + [dma((2, NZ - 1, SLOTS))] * 4,
        compiler_params=pltpu.CompilerParams(
            collective_id=1, has_side_effects=True, vmem_limit_bytes=VMEM_LIMIT
        ),
        name="hidden_grads",
    )(ids, x, w, scale)


def local_kernel(ids, x, w, scale, h, dw, dx):
    def clear(e, carry):
        dw[e] = jnp.zeros((DZ, FP), F32)
        return carry

    lax.fori_loop(0, EXPERTS, clear, 0)
    column = lax.broadcasted_iota(jnp.int32, (DZ, FP), 1)
    nt = (((1,), (1,)), ((), ()))

    def group(i, carry):
        half, gz = i // NZ, i % NZ
        xt = x[half, 0, :, gz].reshape(DZ, TOK)
        dyt = x[half, 1, :, gz].reshape(DZ, TOK).astype(F32)
        total = jnp.zeros((DZ, TOK), F32)
        for slot in range(SLOTS):
            e = ids[i * SLOTS + slot]
            hs = h[gz, half, slot]
            total = total + jnp.dot(
                w[e, :, 0 : 2 * FH], hs[0 : 2 * FH], preferred_element_type=F32
            )
            dys = (dyt * scale[half, gz, pl.ds(slot, 1), :]).astype(BF16)
            gu = lax.dot_general(xt, hs, nt, preferred_element_type=F32)
            dn = lax.dot_general(dys, hs, nt, preferred_element_type=F32)
            dw[e] = dw[e] + jnp.where(column < 2 * FH, gu, dn)
        dx[half, gz] = total
        return carry

    lax.fori_loop(0, NXH * NZ, group, 0)


def local_grads(ids, x, w, scale, h):
    vm = pl.BlockSpec(memory_space=pltpu.VMEM)
    return pl.pallas_call(
        local_kernel,
        out_shape=(
            jax.ShapeDtypeStruct((EXPERTS, DZ, FP), F32),
            jax.ShapeDtypeStruct((NXH, NZ, DZ, TOK), F32),
        ),
        in_specs=[pl.BlockSpec(memory_space=pltpu.SMEM), vm, vm, vm, vm],
        out_specs=(vm, vm),
        compiler_params=pltpu.CompilerParams(vmem_limit_bytes=VMEM_LIMIT),
        name="local_grads",
    )(ids, x, w, scale, h)


def out_kernel(
    dw, dx, wout, xout, wgot, wsnd, wfar, a1, a2, b1, b2, sa, sb, done,
    ts, tr, fs, fr, a1s, a1r, a2s, a2r, b1s, b1r, b2s, b2r, ks, kr,
):
    xl, y, z, xh, c = me = place()
    xp, yp = x_peers(*me), y_peers(*me)
    far = device(xl, y, z, 1 - xh, c)
    twin = device(xl, y, z, xh, 1 - c)
    ex = xl * NY + y
    swap = device(z // NY, z % NY, ex, xh, c)
    barrier = pltpu.get_barrier_semaphore()
    for dev in xp + yp + [twin]:
        pl.semaphore_signal(barrier, inc=1, device_id=dev, device_id_type=MESH)

    @pl.when(ex != z)
    def _():
        pl.semaphore_signal(barrier, inc=1, device_id=swap, device_id_type=MESH)

    pl.semaphore_wait(barrier, 7 + jnp.where(ex != z, 1, 0))

    hd = DZ // 2
    ca = []
    for i in range(3):
        to = (y + i + 1) % NY
        ca.append(
            remote(dx.at[:, :, to, pl.ds(0, hd)], a1.at[i], a1s.at[i], a1r.at[i], yp[i])
        )
        ca[-1].start()
    pos = xh * 2 + xl
    cb = []
    for i in range(3):
        to = (pos + i + 1) % 4
        cb.append(
            remote(
                dx.at[to // 2, to % 2, :, pl.ds(hd, hd)], b1.at[i], b1s.at[i], b1r.at[i], xp[i]
            )
        )
        cb[-1].start()
    ct = []
    for i in range(2):
        blk = (1 - xh) if i == 0 else xh
        ct.append(
            remote(dw.at[:, 2 * blk + 1 - c], wgot.at[i], ts.at[i], tr.at[i], twin)
        )
        ct[-1].start()
    ct[0].wait_recv()

    def add_far(e, carry):
        wsnd[e] = (dw[e, 2 * (1 - xh) + c] + wgot[0, e]).astype(BF16)
        return carry

    lax.fori_loop(0, EXPERTS, add_far, 0)
    cf = remote(wsnd, wfar, fs.at[0], fr.at[0], far)
    cf.start()
    ct[1].wait_recv()

    def add_own(e, carry):
        wout[xh, e] = dw[e, 2 * xh + c] + wgot[1, e]
        return carry

    lax.fori_loop(0, EXPERTS, add_own, 0)

    for k in ca:
        k.wait_recv()
    for i in range(NXH):
        for j in range(NXL):
            sa[i, j] = dx[i, j, y, 0:hd] + a1[0, i, j] + a1[1, i, j] + a1[2, i, j]
    ca2 = []
    for i in range(3):
        to = (pos + i + 1) % 4
        ca2.append(
            remote(sa.at[to // 2, to % 2], a2.at[i], a2s.at[i], a2r.at[i], xp[i])
        )
        ca2[-1].start()
    for k in cb:
        k.wait_recv()
    for j in range(NY):
        sb[j] = dx[xh, xl, j, hd:DZ] + b1[0, j] + b1[1, j] + b1[2, j]
    cb2 = []
    for i in range(3):
        to = (y + i + 1) % NY
        cb2.append(remote(sb.at[to], b2.at[i], b2s.at[i], b2r.at[i], yp[i]))
        cb2[-1].start()
    for k in ca2:
        k.wait_recv()
    done[0:hd] = sa[xh, xl] + a2[0] + a2[1] + a2[2]
    for k in cb2:
        k.wait_recv()
    done[hd:DZ] = sb[y] + b2[0] + b2[1] + b2[2]

    @pl.when(ex != z)
    def _():
        remote(done, xout, ks.at[0], kr.at[0], swap).start()

    @pl.when(ex == z)
    def _():
        xout[...] = done[...]

    cf.wait_recv()

    def widen(e, carry):
        wout[1 - xh, e] = wfar[e].astype(F32)
        return carry

    lax.fori_loop(0, EXPERTS, widen, 0)

    for k in ca + cb + ct + ca2 + cb2 + [cf]:
        k.wait_send()

    @pl.when(ex != z)
    def _():
        remote(done, xout, ks.at[0], kr.at[0], swap).wait()


def exchange_out(dw, dx):
    dma = pltpu.SemaphoreType.DMA
    vm = pl.BlockSpec(memory_space=pltpu.VMEM)
    hd = DZ // 2
    block = (EXPERTS, SUB, FP)
    return pl.pallas_call(
        out_kernel,
        out_shape=(
            jax.ShapeDtypeStruct((NXH, EXPERTS, SUB, FP), F32),
            jax.ShapeDtypeStruct((DZ, TOK), F32),
        ),
        in_specs=[vm, vm],
        out_specs=(vm, vm),
        scratch_shapes=[
            pltpu.VMEM((2,) + block, F32),
            pltpu.VMEM(block, BF16),
            pltpu.VMEM(block, BF16),
            pltpu.VMEM((3, NXH, NXL, hd, TOK), F32),
            pltpu.VMEM((3, hd, TOK), F32),
            pltpu.VMEM((3, NY, hd, TOK), F32),
            pltpu.VMEM((3, hd, TOK), F32),
            pltpu.VMEM((NXH, NXL, hd, TOK), F32),
            pltpu.VMEM((NY, hd, TOK), F32),
            pltpu.VMEM((DZ, TOK), F32),
        ]
        + [dma((2,))] * 2 + [dma((1,))] * 2 + [dma((3,))] * 8 + [dma((1,))] * 2,
        compiler_params=pltpu.CompilerParams(
            collective_id=2, has_side_effects=True, vmem_limit_bytes=VMEM_LIMIT
        ),
        name="exchange_out",
    )(dw, dx)


def shards(
    activations, cotangent, expert_ids, slot_rows, slot_counts, route_probs, w_gate, w_up, w_down
):
    ex = lax.axis_index("expert")
    dp = lax.axis_index("dp")
    xl, y, xh = ex // NY, ex % NY, (dp // 2) % 2

    down_t = w_down.transpose(0, 2, 1)
    wsend = jnp.stack(
        [
            jnp.concatenate(
                [
                    w_gate[:, :, i * FH : (i + 1) * FH],
                    w_up[:, :, i * FH : (i + 1) * FH],
                    down_t[:, :, i * FH : (i + 1) * FH],
                    jnp.zeros((EXPERTS, SUB, FP - F3), BF16),
                ],
                axis=2,
            )
            for i in range(NXH)
        ]
    )

    source = jnp.where(xl == 0, activations, cotangent).reshape(TOK, NZ, NY, SUB)
    piece = lax.dynamic_index_in_dim(source, y, axis=2, keepdims=False).transpose(1, 2, 0)

    position = jnp.arange(TOK, dtype=jnp.int32)
    weight = jnp.where(position[None, :] < slot_counts[0][:, None], route_probs[0], 0.0)
    hit = slot_rows[0][:, :, None] == position[None, None, :]
    row_scale = jnp.sum(jnp.where(hit, weight[:, :, None], 0.0), axis=1)
    info = jnp.concatenate(
        [
            row_scale,
            jnp.broadcast_to(expert_ids[0].astype(F32)[:, None], (SLOTS, TOK)),
            jnp.zeros((4, TOK), F32),
        ]
    )

    x_all, info_all, w_all = exchange(piece, info, wsend)
    ids = info_all[:, :, 2:4, 0].astype(jnp.int32).reshape(-1)
    w_df = w_all.transpose(2, 0, 1, 3, 4).reshape(EXPERTS, DZ, FP)
    w_fd = w_df.transpose(0, 2, 1)
    h = hidden_grads(ids, x_all, w_fd, info_all)
    dw, dx = local_grads(ids, x_all, w_df, info_all, h)
    wout, xout = exchange_out_call(dw, dx)
    grad_gate = jnp.concatenate([wout[0, :, :, 0:FH], wout[1, :, :, 0:FH]], axis=2)
    grad_up = jnp.concatenate(
        [wout[0, :, :, FH : 2 * FH], wout[1, :, :, FH : 2 * FH]], axis=2
    )
    grad_down = jnp.concatenate(
        [wout[0, :, :, 2 * FH : F3], wout[1, :, :, 2 * FH : F3]], axis=2
    ).transpose(0, 2, 1)
    return xout.T, grad_gate, grad_up, grad_down


def exchange_out_call(dw, dx):
    return exchange_out(
        dw.reshape(EXPERTS, NXH * NC, SUB, FP), dx.reshape(NXH, NXL, NY, DZ, TOK)
    )


def solution(mesh):
    return jax.shard_map(
        shards,
        mesh=mesh,
        in_specs=(
            P("dp", None),
            P("dp", None),
            P("dp", None),
            P("dp", None, None),
            P("dp", None),
            P("dp", None, None),
            P(None, "dp", "expert"),
            P(None, "dp", "expert"),
            P(None, "expert", "dp"),
        ),
        out_specs=(
            P("dp", "expert"),
            P(None, "dp", "expert"),
            P(None, "dp", "expert"),
            P(None, "expert", "dp"),
        ),
        check_vma=False,
    )
```

time: 803 us -> 348 us (0.43)
  the two profiles are of different devices: /device:TPU:72 before, /device:TPU:42 now
where the time goes in v1:
time: 348 us
  Pallas kernels  309 us (89%)
  local copies, waits for them, and re-layouts  27.8 us (8%)
  other arithmetic  9.98 us (3%)
    pallas_call x1, Pallas kernels, hidden_grads(): pl.pallas_call(hidden_kernel, out_shape=jax.ShapeDtypeStruct((NZ, NXH, SL...  117 us
    pallas_call x1, Pallas kernels, exchange(): pl.pallas_call(exchange_kernel, out_shape=(jax.ShapeDtypeStruct((NXH, NXL...  90.3 us
    pallas_call x1, Pallas kernels, exchange_out(): pl.pallas_call(out_kernel, out_shape=(jax.ShapeDtypeStruct((NXH, EXPERTS,...  80 us
    pallas_call x1, Pallas kernels, local_grads(): pl.pallas_call(local_kernel, out_shape=(jax.ShapeDtypeStruct((EXPERTS, DZ...  21.9 us
    unnamed x21, local copies, waits for them, and re-layouts  8.51 us

profile of v1, /device:TPU:42, one launch (start us, length us, event | category | flops | bytes accessed | tf_op | source)
XLA Modules:
  0.0 347.7 jit_solution(4302179402302751476)
XLA Ops:
  0.6 0.0 copy-start.3
  0.7 0.7 convert_bitcast_fusion
  1.4 0.1 pad.17.clone
  1.5 0.1 pad.18.clone
  1.5 0.1 pad.15.clone
  1.6 0.8 compare_select_fusion
  2.4 0.8 select_reduce_fusion
  3.2 0.7 maximum_maximum_fusion.info
  3.9 1.1 fusion.1
  5.0 0.2 copy.48
  5.2 0.0 copy-start.2
  5.2 0.2 copy.50
  5.4 0.0 copy-done.3
  5.5 0.2 copy.49
  5.7 0.2 copy.51
  5.9 0.4 copy-done.2
  6.3 0.3 copy.40
  6.6 0.2 fusion
  6.8 1.4 maximum_bitcast_fusion.1
  8.2 0.0 copy-start
  8.2 1.5 pad_maximum_fusion.wsend
  9.7 0.0 copy-done
  9.8 0.0 copy-start.1
  9.8 0.6 copy.36
  10.4 0.6 copy-done.1
  10.9 0.6 copy.37
  11.5 0.1 broadcast_select_fusion
  11.7 0.7 dynamic-slice_bitcast_fusion.piece
  12.4 90.3 %exchange_in.1 = (bf16[2,2,4,8,112,128]{5,4,3,2,1,0:T(8,128)(2,1)}, f32[2,8,8,128]{3,2,1,0:T(8,128)}, bf16[2,2,8,112,464]{4,3,2,1,0:T(8,128)(2,1)}) custom-call(bf16[8,112,128]{2,1,0:T(8,128)(2,1)} %dynamic-slice_bitcast_fusion.piece, f32[8,128]{1,0:T(8,128)} %maximum_maximum_fusion.info, bf16[2,8,112,464]{3,2,1,0:T(8,128)(2,1)} %pad_maximum_fusion.wsend), custom_call_target="tpu_custom_call" | custom-call | tf_op jit(solution)/shard_map/exchange_in/pallas_call | solution.py:127
  102.7 4.2 %copy.43 = bf16[8,2,2,112,464]{4,3,2,1,0:T(8,128)(2,1)} copy(bf16[8,2,2,112,464]{4,3,0,2,1:T(8,128)(2,1)} %bitcast.41) | data formatting | bytes 6651904 | tf_op jit(solution)/shard_map/transpose | solution.py:498
  106.9 1.2 convert_reduce_fusion
  108.1 0.6 convert_element_type.20.ids
  108.7 6.3 %copy.44.w = bf16[8,464,448]{2,1,0:T(8,128)(2,1)} copy(bf16[8,464,448]{1,2,0:T(8,128)(2,1)} %bitcast.37) | data formatting | bytes 6651904 | tf_op jit(solution)/shard_map/transpose | solution.py:499
  115.0 116.9 %hidden_grads.1.h = bf16[8,2,2,464,128]{4,3,2,1,0:T(8,128)(2,1)} custom-call(s32[32]{0:T(128)} %convert_element_type.20.ids, bf16[2,2,4,8,112,128]{5,4,3,2,1,0:T(8,128)(2,1)} %get-tuple-element.12.x, bf16[8,464,448]{2,1,0:T(8,128)(2,1)} %copy.44.w, f32[2,8,8,128]{3,2,1,0:T(8,128)} %get-tuple-element.11.scale), custom_call_target="tpu_custom_call" | custom-call | tf_op jit(solution)/shard_map/hidden_grads/pallas_call | solution.py:249
  231.9 21.9 %local_grads.1 = (f32[8,448,464]{2,1,0:T(8,128)}, f32[2,8,448,128]{3,2,1,0:T(8,128)}) custom-call(s32[32]{0:T(128)} %convert_element_type.20.ids, bf16[2,2,4,8,112,128]{5,4,3,2,1,0:T(8,128)(2,1)} %get-tuple-element.12.x, bf16[8,448,464]{2,1,0:T(8,128)(2,1)} %bitcast.38, f32[2,8,8,128]{3,2,1,0:T(8,128)} %get-tuple-element.11.scale, ...), custom_call_target="tpu_custom_call" | custom-call | tf_op jit(solution)/shard_map/local_grads/pallas_call | solution.py:298
  253.8 80.0 %exchange_out.1 = (f32[2,8,112,464]{3,2,1,0:T(8,128)}, f32[448,128]{1,0:T(8,128)}) custom-call(f32[8,4,112,464]{3,2,1,0:T(8,128)} %bitcast.39, f32[2,2,4,448,128]{4,3,2,1,0:T(8,128)} %bitcast.42), custom_call_target="tpu_custom_call" | custom-call | tf_op jit(solution)/shard_map/exchange_out/pallas_call | solution.py:430
  333.7 5.9 %slice_bitcast_fusion.1 = (f32[8,112,152]{2,1,0:T(8,128)S(1)}, f32[8,112,152]{2,1,0:T(8,128)S(1)}, f32[8,112,152]{2,1,0:T(8,128)}, f32[8,112,152]{2,1,0:T(8,128)...) fusion(f32[2,8,112,464]{3,2,1,0:T(8,128)} %get-tuple-element.17), kind=kLoop, calls=%fused_computation.7 | loop fusion | bytes 6537216 | tf_op jit(solution)/shard_map/squeeze | solution.py:508
  339.6 0.3 maximum_bitcast_fusion
  339.9 1.5 copy.47
  341.4 2.5 pad_maximum_fusion.1
  344.0 1.5 copy.45
  345.5 0.0 copy-start.4
  345.5 1.5 copy.46
  347.0 0.0 copy-done.4
  347.0 0.7 copy.53
  (3 shorter events, 0.1 us)
Async XLA Ops:
  0.6 4.8 %copy-start.3 = (bf16[8,112,304]{1,2,0:T(8,128)(2,1)S(1)}, bf16[8,112,304]{1,2,0:T(8,128)(2,1)}, u32[]{:S(2)}) copy-start(bf16[8,112,304]{1,2,0:T(8,128)(2,1)} %param.16) | copy-start | bytes 1634308
  5.2 1.1 copy-start.2
  8.2 1.5 copy-start
  9.8 1.2 copy-start.1
  345.5 1.5 copy-start.4

commit v2 on v1

v2 whole, which is shorter than its diff:
```python
import jax
import jax.numpy as jnp
from jax import lax
from jax.experimental import pallas as pl
from jax.experimental.pallas import tpu as pltpu
from jax.sharding import PartitionSpec as P

MESH = pl.DeviceIdType.MESH
F32 = jnp.float32
BF16 = jnp.bfloat16

NZ, NXH, NC, NXL, NY = 8, 2, 2, 2, 4
SLOTS = 2
EXPERTS = 8
TOK = 128
SUB = 112
DZ = 448
FH = 152
F3 = 3 * FH
FP = 464
VMEM_LIMIT = 58 * 1024 * 1024


def place():
    ex = lax.axis_index("expert")
    dp = lax.axis_index("dp")
    return ex // NY, ex % NY, dp // 4, (dp // 2) % 2, dp % 2


def device(xl, y, z, xh, c):
    return (xl * NY + y, z * 4 + xh * 2 + c)


def remote(src, dst, ssem, rsem, dev):
    return pltpu.make_async_remote_copy(
        src_ref=src, dst_ref=dst, send_sem=ssem, recv_sem=rsem, device_id=dev, device_id_type=MESH
    )


def greet(devices):
    barrier = pltpu.get_barrier_semaphore()
    for dev in devices:
        pl.semaphore_signal(barrier, inc=1, device_id=dev, device_id_type=MESH)
    pl.semaphore_wait(barrier, len(devices))


def x_peers(xl, y, z, xh, c):
    pos = xh * 2 + xl
    out = []
    for step in range(1, 4):
        to = (pos + step) % 4
        out.append(device(to % 2, y, z, to // 2, c))
    return out


def y_peers(xl, y, z, xh, c):
    return [device(xl, (y + step) % NY, z, xh, c) for step in range(1, NY)]


def z_peers(xl, y, z, xh, c):
    return [device(xl, y, (z + step) % NZ, xh, c) for step in range(1, NZ)]


def exchange_kernel(
    piece, info, wsend, x_out, info_out, w_out, wt_out,
    zs, zr, is_, ir, xs, xr, ixs, ixr, fs, fr, os_, or_, ps, pr, loc,
):
    xl, y, z, xh, c = me = place()
    zp, xp = z_peers(*me), x_peers(*me)
    far = device(xl, y, z, 1 - xh, c)
    twin = device(xl, y, z, xh, 1 - c)
    greet(zp + xp + [twin])
    mine = 2 * xh + c
    other = 2 * (1 - xh) + c

    wfar = []
    for e in range(EXPERTS):
        wfar.append(
            remote(wsend.at[1 - xh, e], w_out.at[e, mine], fs.at[e], fr.at[e], far)
        )
        wfar[-1].start()
    cz = []
    for i in range(NZ - 1):
        to = (z + i + 1) % NZ
        cz.append(remote(piece.at[to], x_out.at[xh, xl, z], zs.at[i], zr.at[i], zp[i]))
        cz[-1].start()
    ci = []
    for i in range(NZ - 1):
        ci.append(remote(info, info_out.at[xh, z], is_.at[i], ir.at[i], zp[i]))
        ci[-1].start()
    wown = []
    for e in range(EXPERTS):
        wown.append(
            remote(wsend.at[xh, e], w_out.at[e, mine], os_.at[e], or_.at[e], twin)
        )
        wown[-1].start()
    here = [
        pltpu.make_async_copy(piece.at[z], x_out.at[xh, xl, z], loc.at[0]),
        pltpu.make_async_copy(info, info_out.at[xh, z], loc.at[1]),
        pltpu.make_async_copy(wsend.at[xh], w_out.at[:, mine], loc.at[2]),
    ]
    for h in here:
        h.start()
    for h in here:
        h.wait()
    for k in cz:
        k.wait()
    cx = []
    for i in range(3):
        cx.append(remote(x_out.at[xh, xl], x_out.at[xh, xl], xs.at[i], xr.at[i], xp[i]))
        cx[-1].start()
    for k in ci:
        k.wait()
    cinf = remote(info_out.at[xh], info_out.at[xh], ixs.at[0], ixr.at[0], far)
    cinf.start()
    wpass = []
    for e in range(EXPERTS):
        wfar[e].wait_recv()
        wpass.append(
            remote(w_out.at[e, other], w_out.at[e, other], ps.at[e], pr.at[e], twin)
        )
        wpass[-1].start()
    for e in range(EXPERTS):
        wown[e].wait_recv()
        wpass[e].wait_recv()
        wt_out[e] = w_out[e].reshape(DZ, FP).T
    for k in cx:
        k.wait()
    cinf.wait()
    for k in wfar + wown + wpass:
        k.wait_send()


def exchange(piece, info, wsend):
    dma = pltpu.SemaphoreType.DMA
    vm = pl.BlockSpec(memory_space=pltpu.VMEM)
    return pl.pallas_call(
        exchange_kernel,
        out_shape=(
            jax.ShapeDtypeStruct((NXH, NXL, NZ, SUB, TOK), BF16),
            jax.ShapeDtypeStruct((NXH, NZ, 8, TOK), F32),
            jax.ShapeDtypeStruct((EXPERTS, NXH * NC, SUB, FP), BF16),
            jax.ShapeDtypeStruct((EXPERTS, FP, DZ), BF16),
        ),
        in_specs=[vm] * 3,
        out_specs=(vm,) * 4,
        scratch_shapes=[dma((7,))] * 4 + [dma((3,))] * 2 + [dma((1,))] * 2 + [dma((EXPERTS,))] * 6
        + [dma((3,))],
        compiler_params=pltpu.CompilerParams(
            collective_id=0, has_side_effects=True, vmem_limit_bytes=VMEM_LIMIT
        ),
        name="exchange_in",
    )(piece, info, wsend)


def layer_kernel(
    ids, xin, w, wt, scale, wout, xout,
    x, acc, own, h, xcat, dcat, hcat, dx, dw, wgot, wsnd, wfar, a1, a2, b1, b2, sa, sb, done,
    loc, y_s, y_r, rs_s, rs_r, ag_s, ag_r,
    a1s, a1r, b1s, b1r, a2s, a2r, b2s, b2r, ts, tr, fs, fr, ks, kr,
):
    xl, y, z, xh, c = me = place()
    ex = xl * NY + y
    pos = xh * 2 + xl
    hd = DZ // 2
    xp, yp = x_peers(*me), y_peers(*me)
    up = device(xl, y, (z + 1) % NZ, xh, c)
    down = device(xl, y, (z + NZ - 1) % NZ, xh, c)
    to = (up, down)
    far = device(xl, y, z, 1 - xh, c)
    twin = device(xl, y, z, xh, 1 - c)
    swap = device(z // NY, z % NY, ex, xh, c)
    barrier = pltpu.get_barrier_semaphore()
    for dev in xp + yp + [up, down, twin]:
        pl.semaphore_signal(barrier, inc=1, device_id=dev, device_id_type=MESH)

    @pl.when(ex != z)
    def _():
        pl.semaphore_signal(barrier, inc=1, device_id=swap, device_id_type=MESH)

    pl.semaphore_wait(barrier, 9 + jnp.where(ex != z, 1, 0))

    def chunk(half, s):
        return (z + 2 * NZ - 1 - s) % NZ if half == 0 else (z + 1 + s) % NZ

    def spread(half, s, i):
        gz = chunk(half, s)
        return remote(
            xin.at[half, :, gz], x.at[half, :, y, gz], y_s.at[half, s, i], y_r.at[half, s, i], yp[i]
        )

    def spread_all(s):
        for half in range(2):
            for i in range(3):
                spread(half, s, i).start()

    def await_all(s):
        for half in range(2):
            for i in range(3):
                spread(half, s, i).wait_recv()

    keep = pltpu.make_async_copy(xin, x.at[:, :, y], loc.at[0])
    keep.start()
    spread_all(0)
    spread_all(1)
    keep.wait()

    def partial(half, gz):
        lanes = pl.ds(pl.multiple_of((half * NZ + gz) * TOK, TOK), TOK)
        xt = x[half, 0, :, gz].reshape(DZ, TOK)
        dyt = x[half, 1, :, gz].reshape(DZ, TOK).astype(F32)
        xcat[:, lanes] = xt
        for slot in range(SLOTS):
            e = ids[half * (NZ * SLOTS) + gz * SLOTS + slot]
            dys = (dyt * scale[half, gz, pl.ds(slot, 1), :]).astype(BF16)
            dcat[slot, :, lanes] = dys
            gu = jnp.dot(wt[e, 0 : 2 * FH, :], xt, preferred_element_type=F32)
            dh = jnp.dot(wt[e, 2 * FH : FP, :], dys, preferred_element_type=F32)
            own[half, slot, 0 : 2 * FH, :] = gu
            own[half, slot, 2 * FH : F3, :] = dh[:FH]

    def hop(half, slot, s, src):
        return remote(
            src, acc.at[half, s, slot], rs_s.at[half, s, slot], rs_r.at[half, s, slot], to[half]
        )

    await_all(0)
    for half in range(2):
        partial(half, chunk(half, 0))
        for slot in range(SLOTS):
            hop(half, slot, 0, own.at[half, slot]).start()
    for half in range(2):
        for slot in range(SLOTS):
            hop(half, slot, 0, own.at[half, slot]).wait_send()

    def ring(s, carry):
        spread_all(s + 1)
        await_all(s)
        for half in range(2):
            partial(half, chunk(half, s))
        for slot in range(SLOTS):
            for half in range(2):
                here = acc.at[half, s - 1, slot]
                hop(half, slot, s - 1, here).wait_recv()
                acc[half, s - 1, slot] = acc[half, s - 1, slot] + own[half, slot]
                hop(half, slot, s, here).start()
        return carry

    lax.fori_loop(1, NZ - 1, ring, 0)
    await_all(NZ - 1)

    def gather(half, slot, s, gz):
        ref = h.at[gz, half, slot]
        return remote(ref, ref, ag_s.at[half, s, slot], ag_r.at[half, s, slot], to[half])

    def origin(half, s):
        return (z + NZ - s) % NZ if half == 0 else (z + s) % NZ

    def rows_a(half, gz):
        i = (gz % NY - y + NY) % NY
        src = dx.at[half, gz // NY, gz % NY, pl.ds(0, hd)]
        return i, lambda: remote(
            src, a1.at[i - 1, half, gz // NY], a1s.at[half, gz], a1r.at[i - 1, half, gz // NY],
            device(xl, gz % NY, z, xh, c),
        )

    def rows_b(half, gz):
        i = (half * 2 + gz // NY - pos + 4) % 4
        src = dx.at[half, gz // NY, gz % NY, pl.ds(hd, hd)]
        return i, lambda: remote(
            src, b1.at[i - 1, gz % NY], b1s.at[half, gz], b1r.at[i - 1, gz % NY],
            device(gz // NY, y, z, half, c),
        )

    def rows(half, gz):
        lanes = pl.ds(pl.multiple_of((half * NZ + gz) * TOK, TOK), TOK)
        total = jnp.zeros((DZ, TOK), F32)
        for slot in range(SLOTS):
            e = ids[half * (NZ * SLOTS) + gz * SLOTS + slot]
            hs = h[gz, half, slot]
            hcat[slot, :, lanes] = hs
            total = total + jnp.dot(
                w[e, :, 0 : 2 * FH], hs[0 : 2 * FH], preferred_element_type=F32
            )
        dx[half, gz // NY, gz % NY] = total
        for i, make in (rows_a(half, gz), rows_b(half, gz)):

            @pl.when(i != 0)
            def _(make=make):
                make().start()

    for half in range(2):
        partial(half, z)
    for slot in range(SLOTS):
        for half in range(2):
            last = acc.at[half, NZ - 2, slot]
            hop(half, slot, NZ - 2, last).wait_recv()
            g = acc[half, NZ - 2, slot, 0:FH, :] + own[half, slot, 0:FH, :]
            u = acc[half, NZ - 2, slot, FH : 2 * FH, :] + own[half, slot, FH : 2 * FH, :]
            dh = acc[half, NZ - 2, slot, 2 * FH : F3, :] + own[half, slot, 2 * FH : F3, :]
            sig = 1.0 / (1.0 + jnp.exp(-g))
            act = g * sig
            dg = dh * u * sig * (1.0 + g * (1.0 - sig))
            du = dh * act
            hid = act * u
            h[z, half, slot, 0 : 2 * FH, :] = jnp.concatenate([dg, du], axis=0).astype(BF16)
            h[z, half, slot, 2 * FH : FP, :] = jnp.concatenate(
                [hid, jnp.zeros((FP - F3, TOK), F32)], axis=0
            ).astype(BF16)
            gather(half, slot, 0, z).start()
    for half in range(2):
        rows(half, z)

    def pass_on(s, carry):
        for slot in range(SLOTS):
            for half in range(2):
                gather(half, slot, s - 1, origin(half, s)).wait_recv()
                gather(half, slot, s, origin(half, s)).start()
        for half in range(2):
            rows(half, origin(half, s))
        return carry

    lax.fori_loop(1, NZ - 1, pass_on, 0)
    for half in range(2):
        for slot in range(SLOTS):
            gather(half, slot, NZ - 2, origin(half, NZ - 1)).wait_recv()
        rows(half, origin(half, NZ - 1))

    cols = NXH * NZ * TOK
    def expert_row(slot):
        return jnp.concatenate(
            [
                scale[i // NZ, i % NZ, 2 + slot : 3 + slot, :]
                for i in range(NXH * NZ)
            ],
            axis=1,
        )

    id0, id1 = expert_row(0), expert_row(1)
    nt = (((1,), (1,)), ((), ()))

    def weights(e):
        is0 = jnp.broadcast_to(id0 == e.astype(F32), (16, cols))
        is1 = jnp.broadcast_to(id1 == e.astype(F32), (16, cols))
        zero = jnp.zeros((16, cols), BF16)

        def pick(pair, n):
            return jnp.concatenate(
                [
                    jnp.where(
                        is0,
                        pair[0, r * 16 : (r + 1) * 16, :],
                        jnp.where(is1, pair[1, r * 16 : (r + 1) * 16, :], zero),
                    )
                    for r in range(n // 16)
                ],
                axis=0,
            )

        hs = pick(hcat, FP)
        ds = pick(dcat, DZ)
        gu = lax.dot_general(xcat[...], hs, nt, preferred_element_type=F32)
        dn = lax.dot_general(ds, hs[256:], nt, preferred_element_type=F32)
        column = lax.broadcasted_iota(jnp.int32, (DZ, FP - 256), 1)
        tail = jnp.where(column < 2 * FH - 256, gu[:, 256:], dn)
        for q in range(NXH * NC):
            dw[e, q, :, 0:256] = gu[q * SUB : (q + 1) * SUB, 0:256]
            dw[e, q, :, 256:FP] = tail[q * SUB : (q + 1) * SUB]

    def cross(e, i):
        blk = (1 - xh) if i == 0 else xh
        return remote(dw.at[e, 2 * blk + 1 - c], wgot.at[i, e], ts.at[i, e], tr.at[i, e], twin)

    def away(e):
        return remote(wsnd.at[e], wfar.at[e], fs.at[e], fr.at[e], far)

    def combine(e):
        cross(e, 0).wait_recv()
        wsnd[e] = (dw[e, 2 * (1 - xh) + c] + wgot[0, e]).astype(BF16)
        away(e).start()
        cross(e, 1).wait_recv()
        wout[xh, e] = dw[e, 2 * xh + c] + wgot[1, e]

    def per_expert(e, carry):
        weights(e)
        cross(e, 0).start()
        cross(e, 1).start()

        @pl.when(e > 0)
        def _():
            combine(e - 1)

        return carry

    lax.fori_loop(0, EXPERTS, per_expert, 0)
    combine(EXPERTS - 1)

    for i in range(3):
        for j in range(NXH):
            for k in range(NXL):
                remote(
                    dx.at[0, 0, 0, pl.ds(0, hd)], a1.at[i, j, k], a1s.at[0, 0], a1r.at[i, j, k], up
                ).wait_recv()
    for j in range(NXH):
        for k in range(NXL):
            sa[j, k] = dx[j, k, y, 0:hd] + a1[0, j, k] + a1[1, j, k] + a1[2, j, k]
    ca2 = []
    for i in range(3):
        t = (pos + i + 1) % 4
        ca2.append(remote(sa.at[t // 2, t % 2], a2.at[i], a2s.at[i], a2r.at[i], xp[i]))
        ca2[-1].start()
    for i in range(3):
        for j in range(NY):
            remote(
                dx.at[0, 0, 0, pl.ds(hd, hd)], b1.at[i, j], b1s.at[0, 0], b1r.at[i, j], up
            ).wait_recv()
    for j in range(NY):
        sb[j] = dx[xh, xl, j, hd:DZ] + b1[0, j] + b1[1, j] + b1[2, j]
    cb2 = []
    for i in range(3):
        t = (y + i + 1) % NY
        cb2.append(remote(sb.at[t], b2.at[i], b2s.at[i], b2r.at[i], yp[i]))
        cb2[-1].start()
    for k in ca2:
        k.wait_recv()
    done[0:hd] = sa[xh, xl] + a2[0] + a2[1] + a2[2]
    for k in cb2:
        k.wait_recv()
    done[hd:DZ] = sb[y] + b2[0] + b2[1] + b2[2]

    @pl.when(ex != z)
    def _():
        remote(done, xout, ks.at[0], kr.at[0], swap).start()

    @pl.when(ex == z)
    def _():
        xout[...] = done[...]

    def widen(e, carry):
        away(e).wait_recv()
        wout[1 - xh, e] = wfar[e].astype(F32)
        return carry

    lax.fori_loop(0, EXPERTS, widen, 0)

    def drain_ring(s, carry):
        for half in range(2):
            for slot in range(SLOTS):
                hop(half, slot, s, acc.at[half, s - 1, slot]).wait_send()
                gather(half, slot, s, origin(half, s)).wait_send()
        return carry

    lax.fori_loop(1, NZ - 1, drain_ring, 0)
    for half in range(2):
        for slot in range(SLOTS):
            gather(half, slot, 0, z).wait_send()

    def drain(s, carry):
        for half in range(2):
            for i in range(3):
                spread(half, s, i).wait_send()
            for i, make in (rows_a(half, s), rows_b(half, s)):

                @pl.when(i != 0)
                def _(make=make):
                    make().wait_send()

        cross(s, 0).wait_send()
        cross(s, 1).wait_send()
        away(s).wait_send()
        return carry

    lax.fori_loop(0, NZ, drain, 0)
    for k in ca2 + cb2:
        k.wait_send()

    @pl.when(ex != z)
    def _():
        remote(done, xout, ks.at[0], kr.at[0], swap).wait()


def layer(ids, xin, w, wt, scale):
    dma = pltpu.SemaphoreType.DMA
    vm = pl.BlockSpec(memory_space=pltpu.VMEM)
    hd = DZ // 2
    cols = NXH * NZ * TOK
    block = (EXPERTS, SUB, FP)
    return pl.pallas_call(
        layer_kernel,
        out_shape=(
            jax.ShapeDtypeStruct((NXH, EXPERTS, SUB, FP), F32),
            jax.ShapeDtypeStruct((DZ, TOK), F32),
        ),
        in_specs=[pl.BlockSpec(memory_space=pltpu.SMEM), vm, vm, vm, vm],
        out_specs=(vm, vm),
        scratch_shapes=[
            pltpu.VMEM((NXH, NXL, NY, NZ, SUB, TOK), BF16),
            pltpu.VMEM((2, NZ - 1, SLOTS, F3, TOK), F32),
            pltpu.VMEM((2, SLOTS, F3, TOK), F32),
            pltpu.VMEM((NZ, NXH, SLOTS, FP, TOK), BF16),
            pltpu.VMEM((DZ, cols), BF16),
            pltpu.VMEM((SLOTS, DZ, cols), BF16),
            pltpu.VMEM((SLOTS, FP, cols), BF16),
            pltpu.VMEM((NXH, NXL, NY, DZ, TOK), F32),
            pltpu.VMEM((EXPERTS, NXH * NC, SUB, FP), F32),
            pltpu.VMEM((2,) + block, F32),
            pltpu.VMEM(block, BF16),
            pltpu.VMEM(block, BF16),
            pltpu.VMEM((3, NXH, NXL, hd, TOK), F32),
            pltpu.VMEM((3, hd, TOK), F32),
            pltpu.VMEM((3, NY, hd, TOK), F32),
            pltpu.VMEM((3, hd, TOK), F32),
            pltpu.VMEM((NXH, NXL, hd, TOK), F32),
            pltpu.VMEM((NY, hd, TOK), F32),
            pltpu.VMEM((DZ, TOK), F32),
            dma((1,)),
            dma((2, NZ, 3)),
            dma((2, NZ, 3)),
        ]
        + [dma((2, NZ - 1, SLOTS))] * 4
        + [dma((2, NZ)), dma((3, NXH, NXL)), dma((2, NZ)), dma((3, NY))]
        + [dma((3,))] * 4
        + [dma((2, EXPERTS))] * 2
        + [dma((EXPERTS,))] * 2
        + [dma((1,))] * 2,
        compiler_params=pltpu.CompilerParams(
            collective_id=1, has_side_effects=True, vmem_limit_bytes=VMEM_LIMIT
        ),
        name="layer",
    )(ids, xin, w, wt, scale)


def shards(
    activations, cotangent, expert_ids, slot_rows, slot_counts, route_probs, w_gate, w_up, w_down
):
    ex = lax.axis_index("expert")
    dp = lax.axis_index("dp")
    xl, y, xh = ex // NY, ex % NY, (dp // 2) % 2

    down_t = w_down.transpose(0, 2, 1)
    wsend = jnp.stack(
        [
            jnp.concatenate(
                [
                    w_gate[:, :, i * FH : (i + 1) * FH],
                    w_up[:, :, i * FH : (i + 1) * FH],
                    down_t[:, :, i * FH : (i + 1) * FH],
                    jnp.zeros((EXPERTS, SUB, FP - F3), BF16),
                ],
                axis=2,
            )
            for i in range(NXH)
        ]
    )

    source = jnp.where(xl == 0, activations, cotangent).reshape(TOK, NZ, NY, SUB)
    piece = lax.dynamic_index_in_dim(source, y, axis=2, keepdims=False).transpose(1, 2, 0)

    position = jnp.arange(TOK, dtype=jnp.int32)
    weight = jnp.where(position[None, :] < slot_counts[0][:, None], route_probs[0], 0.0)
    hit = slot_rows[0][:, :, None] == position[None, None, :]
    row_scale = jnp.sum(jnp.where(hit, weight[:, :, None], 0.0), axis=1)
    info = jnp.concatenate(
        [
            row_scale,
            jnp.broadcast_to(expert_ids[0].astype(F32)[:, None], (SLOTS, TOK)),
            jnp.zeros((4, TOK), F32),
        ]
    )

    xin, info_all, w_all, wt = exchange(piece, info, wsend)
    ids = info_all[:, :, 2:4, 0].astype(jnp.int32).reshape(-1)
    wout, xout = layer(ids, xin, w_all.reshape(EXPERTS, DZ, FP), wt, info_all)
    grad_gate = jnp.concatenate([wout[0, :, :, 0:FH], wout[1, :, :, 0:FH]], axis=2)
    grad_up = jnp.concatenate(
        [wout[0, :, :, FH : 2 * FH], wout[1, :, :, FH : 2 * FH]], axis=2
    )
    grad_down = jnp.concatenate(
        [wout[0, :, :, 2 * FH : F3], wout[1, :, :, 2 * FH : F3]], axis=2
    ).transpose(0, 2, 1)
    return xout.T, grad_gate, grad_up, grad_down


def solution(mesh):
    return jax.shard_map(
        shards,
        mesh=mesh,
        in_specs=(
            P("dp", None),
            P("dp", None),
            P("dp", None),
            P("dp", None, None),
            P("dp", None),
            P("dp", None, None),
            P(None, "dp", "expert"),
            P(None, "dp", "expert"),
            P(None, "expert", "dp"),
        ),
        out_specs=(
            P("dp", "expert"),
            P(None, "dp", "expert"),
            P(None, "dp", "expert"),
            P(None, "expert", "dp"),
        ),
        check_vma=False,
    )
```

time: 348 us -> 260 us (0.75)
  the two profiles are of different devices: /device:TPU:42 before, /device:TPU:64 now
where the time goes in v2:
time: 260 us
  Pallas kernels  232 us (89%)
  local copies, waits for them, and re-layouts  17.2 us (7%)
  other arithmetic  9.95 us (4%)
    pallas_call x1, Pallas kernels, layer(): pl.pallas_call(layer_kernel, out_shape=(jax.ShapeDtypeStruct((NXH, EXPERT...  187 us
    pallas_call x1, Pallas kernels, exchange(): pl.pallas_call(exchange_kernel, out_shape=(jax.ShapeDtypeStruct((NXH, NXL...  44.8 us
    unnamed x21, local copies, waits for them, and re-layouts  8.51 us
    squeeze x1, local copies, waits for them, and re-layouts, shards(): wout[0, :, :, 2 * FH:F3]  5.8 us

profile of v2, /device:TPU:64, one launch (start us, length us, event | category | flops | bytes accessed | tf_op | source)
XLA Modules:
  0.0 259.6 jit_solution(7794360530050157745)
XLA Ops:
  0.6 0.0 copy-start.3
  0.7 0.7 convert_bitcast_fusion
  1.4 0.1 pad.17.clone
  1.5 0.1 pad.18.clone
  1.5 0.1 pad.15.clone
  1.6 0.8 compare_select_fusion
  2.4 0.8 select_reduce_fusion
  3.2 0.7 maximum_maximum_fusion.info
  3.9 1.1 fusion.1
  5.0 0.2 copy.42
  5.2 0.0 copy-start.2
  5.2 0.2 copy.44
  5.4 0.0 copy-done.3
  5.5 0.2 copy.43
  5.7 0.2 copy.45
  5.9 0.4 copy-done.2
  6.3 0.3 copy.36
  6.6 0.2 fusion
  6.8 1.4 maximum_bitcast_fusion.1
  8.2 0.0 copy-start
  8.2 1.5 pad_maximum_fusion.wsend
  9.7 0.0 copy-done
  9.7 0.0 copy-start.1
  9.7 0.6 copy.32
  10.3 0.6 copy-done.1
  10.9 0.6 copy.33
  11.5 0.1 broadcast_select_fusion
  11.6 0.7 dynamic-slice_bitcast_fusion.piece
  12.3 44.8 %exchange_in.1 = (bf16[2,2,8,112,128]{4,3,2,1,0:T(8,128)(2,1)}, f32[2,8,8,128]{3,2,1,0:T(8,128)}, bf16[8,4,112,464]{3,2,1,0:T(8,128)(2,1)}, bf16[8,464,448]{2,1,0:T(8,128)(2,1)}) custom-call(bf16[8,112,128]{2,1,0:T(8,128)(2,1)} %dynamic-slice_bitcast_fusion.piece, f32[8,128]{1,0:T(8,128)} %maximum_maximum_fusion.info, ...), custom_call_target="tpu_custom_call" | custom-call | tf_op jit(solution)/shard_map/exchange_in/pallas_call | solution.py:137
  57.1 1.2 convert_reduce_fusion
  58.3 0.6 convert_element_type.20.ids
  58.9 186.9 %layer.1 = (f32[2,8,112,464]{3,2,1,0:T(8,128)}, f32[448,128]{1,0:T(8,128)}) custom-call(s32[32]{0:T(128)} %convert_element_type.20.ids, bf16[2,2,8,112,128]{4,3,2,1,0:T(8,128)(2,1)} %get-tuple-element.11.xin, bf16[8,448,464]{2,1,0:T(8,128)(2,1)} %bitcast.33, bf16[8,464,448]{2,1,0:T(8,128)(2,1)} %get-tuple-element.13.wt, f32[2,8,8,128]{3,2,1,0:T(8,128)} %get-tuple-element.10.scale), custom_call_target="tpu_custom_call" | custom-call | tf_op jit(solution)/shard_map/layer/pallas_call | solution.py:488
  245.8 5.8 %slice_bitcast_fusion.1 = (f32[8,112,152]{2,1,0:T(8,128)S(1)}, f32[8,112,152]{2,1,0:T(8,128)S(1)}, f32[8,112,152]{2,1,0:T(8,128)}, f32[8,112,152]{2,1,0:T(8,128)...) fusion(f32[2,8,112,464]{3,2,1,0:T(8,128)} %get-tuple-element.15), kind=kLoop, calls=%fused_computation.7 | loop fusion | bytes 6537216 | tf_op jit(solution)/shard_map/squeeze | solution.py:579
  251.6 0.3 maximum_bitcast_fusion
  251.9 1.5 copy.41
  253.4 2.5 pad_maximum_fusion.1
  256.0 1.5 copy.39
  257.5 0.0 copy-start.4
  257.5 1.5 copy.40
  259.0 0.0 copy-done.4
  259.0 0.7 copy.47
  (3 shorter events, 0.1 us)
Async XLA Ops:
  0.6 4.8 %copy-start.3 = (bf16[8,112,304]{1,2,0:T(8,128)(2,1)S(1)}, bf16[8,112,304]{1,2,0:T(8,128)(2,1)}, u32[]{:S(2)}) copy-start(bf16[8,112,304]{1,2,0:T(8,128)(2,1)} %param.16) | copy-start | bytes 1634308
  5.2 1.1 copy-start.2
  8.2 1.5 copy-start
  9.7 1.2 copy-start.1
  257.5 1.5 copy-start.4

commit v3 on v2

--- a/solution.py
+++ b/solution.py
@@ -63,13 +63,14 @@
 
 def exchange_kernel(
     piece, info, wsend, x_out, info_out, w_out, wt_out,
-    zs, zr, is_, ir, xs, xr, ixs, ixr, fs, fr, os_, or_, ps, pr, loc,
+    zs, zr, is_, ir, ys, yr, ixs, ixr, fs, fr, os_, or_, ps, pr, loc,
 ):
     xl, y, z, xh, c = me = place()
-    zp, xp = z_peers(*me), x_peers(*me)
+    zp, yp = z_peers(*me), y_peers(*me)
     far = device(xl, y, z, 1 - xh, c)
     twin = device(xl, y, z, xh, 1 - c)
-    greet(zp + xp + [twin])
+    greet(zp + yp + [far, twin])
+    part = pl.ds(pl.multiple_of(y * SUB, SUB), SUB)
     mine = 2 * xh + c
     other = 2 * (1 - xh) + c
 
@@ -82,7 +83,7 @@
     cz = []
     for i in range(NZ - 1):
         to = (z + i + 1) % NZ
-        cz.append(remote(piece.at[to], x_out.at[xh, xl, z], zs.at[i], zr.at[i], zp[i]))
+        cz.append(remote(piece.at[to], x_out.at[z, part], zs.at[i], zr.at[i], zp[i]))
         cz[-1].start()
     ci = []
     for i in range(NZ - 1):
@@ -95,7 +96,7 @@
         )
         wown[-1].start()
     here = [
-        pltpu.make_async_copy(piece.at[z], x_out.at[xh, xl, z], loc.at[0]),
+        pltpu.make_async_copy(piece.at[z], x_out.at[z, part], loc.at[0]),
         pltpu.make_async_copy(info, info_out.at[xh, z], loc.at[1]),
         pltpu.make_async_copy(wsend.at[xh], w_out.at[:, mine], loc.at[2]),
     ]
@@ -105,10 +106,10 @@
         h.wait()
     for k in cz:
         k.wait()
-    cx = []
+    cy = []
     for i in range(3):
-        cx.append(remote(x_out.at[xh, xl], x_out.at[xh, xl], xs.at[i], xr.at[i], xp[i]))
-        cx[-1].start()
+        cy.append(remote(x_out.at[:, part], x_out.at[:, part], ys.at[i], yr.at[i], yp[i]))
+        cy[-1].start()
     for k in ci:
         k.wait()
     cinf = remote(info_out.at[xh], info_out.at[xh], ixs.at[0], ixr.at[0], far)
@@ -124,7 +125,7 @@
         wown[e].wait_recv()
         wpass[e].wait_recv()
         wt_out[e] = w_out[e].reshape(DZ, FP).T
-    for k in cx:
+    for k in cy:
         k.wait()
     cinf.wait()
     for k in wfar + wown + wpass:
@@ -137,7 +138,7 @@
     return pl.pallas_call(
         exchange_kernel,
         out_shape=(
-            jax.ShapeDtypeStruct((NXH, NXL, NZ, SUB, TOK), BF16),
+            jax.ShapeDtypeStruct((NZ, DZ, TOK), BF16),
             jax.ShapeDtypeStruct((NXH, NZ, 8, TOK), F32),
             jax.ShapeDtypeStruct((EXPERTS, NXH * NC, SUB, FP), BF16),
             jax.ShapeDtypeStruct((EXPERTS, FP, DZ), BF16),
@@ -154,9 +155,9 @@
 
 
 def layer_kernel(
-    ids, xin, w, wt, scale, wout, xout,
-    x, acc, own, h, xcat, dcat, hcat, dx, dw, wgot, wsnd, wfar, a1, a2, b1, b2, sa, sb, done,
-    loc, y_s, y_r, rs_s, rs_r, ag_s, ag_r,
+    ids, xin, w, wt, scale, gate, up_out, down_out, xout,
+    x, acc, own, dcat, hcat, dx, dw, wgot, wsnd, wfar, a1, a2, b1, b2, sa, sb, done, back,
+    x_s, x_r, rs_s, rs_r, ag_s, ag_r,
     a1s, a1r, b1s, b1r, a2s, a2r, b2s, b2r, ts, tr, fs, fr, ks, kr,
 ):
     xl, y, z, xh, c = me = place()
@@ -180,40 +181,39 @@
 
     pl.semaphore_wait(barrier, 9 + jnp.where(ex != z, 1, 0))
 
+    def lanes(half, gz):
+        return pl.ds(pl.multiple_of((half * NZ + gz) * TOK, TOK), TOK)
+
     def chunk(half, s):
-        return (z + 2 * NZ - 1 - s) % NZ if half == 0 else (z + 1 + s) % NZ
-
-    def spread(half, s, i):
-        gz = chunk(half, s)
+        return jnp.where(half == 0, z + 2 * NZ - 1 - s, z + 1 + s) % NZ
+
+    def spread(s, i):
+        gz = chunk(xh, s)
         return remote(
-            xin.at[half, :, gz], x.at[half, :, y, gz], y_s.at[half, s, i], y_r.at[half, s, i], yp[i]
+            xin.at[gz], x.at[xl, :, lanes(xh, gz)], x_s.at[s, i], x_r.at[s, i], xp[i]
         )
 
     def spread_all(s):
-        for half in range(2):
-            for i in range(3):
-                spread(half, s, i).start()
+        for i in range(3):
+            spread(s, i).start()
 
     def await_all(s):
-        for half in range(2):
-            for i in range(3):
-                spread(half, s, i).wait_recv()
-
-    keep = pltpu.make_async_copy(xin, x.at[:, :, y], loc.at[0])
-    keep.start()
+        gz = chunk(xh, s)
+        x[xl, :, lanes(xh, gz)] = xin[gz]
+        for i in range(3):
+            spread(s, i).wait_recv()
+
     spread_all(0)
     spread_all(1)
-    keep.wait()
 
     def partial(half, gz):
-        lanes = pl.ds(pl.multiple_of((half * NZ + gz) * TOK, TOK), TOK)
-        xt = x[half, 0, :, gz].reshape(DZ, TOK)
-        dyt = x[half, 1, :, gz].reshape(DZ, TOK).astype(F32)
-        xcat[:, lanes] = xt
+        at = lanes(half, gz)
+        xt = x[0, :, at]
+        dyt = x[1, :, at].astype(F32)
         for slot in range(SLOTS):
             e = ids[half * (NZ * SLOTS) + gz * SLOTS + slot]
             dys = (dyt * scale[half, gz, pl.ds(slot, 1), :]).astype(BF16)
-            dcat[slot, :, lanes] = dys
+            dcat[slot, :, at] = dys
             gu = jnp.dot(wt[e, 0 : 2 * FH, :], xt, preferred_element_type=F32)
             dh = jnp.dot(wt[e, 2 * FH : FP, :], dys, preferred_element_type=F32)
             own[half, slot, 0 : 2 * FH, :] = gu
@@ -250,7 +250,7 @@
     await_all(NZ - 1)
 
     def gather(half, slot, s, gz):
-        ref = h.at[gz, half, slot]
+        ref = hcat.at[slot, :, lanes(half, gz)]
         return remote(ref, ref, ag_s.at[half, s, slot], ag_r.at[half, s, slot], to[half])
 
     def origin(half, s):
@@ -273,14 +273,12 @@
         )
 
     def rows(half, gz):
-        lanes = pl.ds(pl.multiple_of((half * NZ + gz) * TOK, TOK), TOK)
         total = jnp.zeros((DZ, TOK), F32)
         for slot in range(SLOTS):
             e = ids[half * (NZ * SLOTS) + gz * SLOTS + slot]
-            hs = h[gz, half, slot]
-            hcat[slot, :, lanes] = hs
+            hs = hcat[slot, 0 : 2 * FH, lanes(half, gz)]
             total = total + jnp.dot(
-                w[e, :, 0 : 2 * FH], hs[0 : 2 * FH], preferred_element_type=F32
+                w[e, :, 0 : 2 * FH], hs, preferred_element_type=F32
             )
         dx[half, gz // NY, gz % NY] = total
         for i, make in (rows_a(half, gz), rows_b(half, gz)):
@@ -303,8 +301,8 @@
             dg = dh * u * sig * (1.0 + g * (1.0 - sig))
             du = dh * act
             hid = act * u
-            h[z, half, slot, 0 : 2 * FH, :] = jnp.concatenate([dg, du], axis=0).astype(BF16)
-            h[z, half, slot, 2 * FH : FP, :] = jnp.concatenate(
+            hcat[slot, 0 : 2 * FH, lanes(half, z)] = jnp.concatenate([dg, du], axis=0).astype(BF16)
+            hcat[slot, 2 * FH : FP, lanes(half, z)] = jnp.concatenate(
                 [hid, jnp.zeros((FP - F3, TOK), F32)], axis=0
             ).astype(BF16)
             gather(half, slot, 0, z).start()
@@ -359,7 +357,7 @@
 
         hs = pick(hcat, FP)
         ds = pick(dcat, DZ)
-        gu = lax.dot_general(xcat[...], hs, nt, preferred_element_type=F32)
+        gu = lax.dot_general(x[0], hs, nt, preferred_element_type=F32)
         dn = lax.dot_general(ds, hs[256:], nt, preferred_element_type=F32)
         column = lax.broadcasted_iota(jnp.int32, (DZ, FP - 256), 1)
         tail = jnp.where(column < 2 * FH - 256, gu[:, 256:], dn)
@@ -379,7 +377,63 @@
         wsnd[e] = (dw[e, 2 * (1 - xh) + c] + wgot[0, e]).astype(BF16)
         away(e).start()
         cross(e, 1).wait_recv()
-        wout[xh, e] = dw[e, 2 * xh + c] + wgot[1, e]
+        wgot[1, e] = dw[e, 2 * xh + c] + wgot[1, e]
+
+    def second(i, kind):
+        if kind == 0:
+            t = (pos + i + 1) % 4
+            return remote(sa.at[t // 2, t % 2], a2.at[i], a2s.at[i], a2r.at[i], xp[i])
+        t = (y + i + 1) % NY
+        return remote(sb.at[t], b2.at[i], b2s.at[i], b2r.at[i], yp[i])
+
+    def rows_second():
+        for i in range(3):
+            for j in range(NXH):
+                for k in range(NXL):
+                    remote(
+                        dx.at[0, 0, 0, pl.ds(0, hd)], a1.at[i, j, k], a1s.at[0, 0],
+                        a1r.at[i, j, k], up,
+                    ).wait_recv()
+        for j in range(NXH):
+            for k in range(NXL):
+                sa[j, k] = dx[j, k, y, 0:hd] + a1[0, j, k] + a1[1, j, k] + a1[2, j, k]
+        for i in range(3):
+            second(i, 0).start()
+        for i in range(3):
+            for j in range(NY):
+                remote(
+                    dx.at[0, 0, 0, pl.ds(hd, hd)], b1.at[i, j], b1s.at[0, 0], b1r.at[i, j], up
+                ).wait_recv()
+        for j in range(NY):
+            sb[j] = dx[xh, xl, j, hd:DZ] + b1[0, j] + b1[1, j] + b1[2, j]
+        for i in range(3):
+            second(i, 1).start()
+
+    def rows_swap():
+        for i in range(3):
+            second(i, 0).wait_recv()
+        done[0:hd] = sa[xh, xl] + a2[0] + a2[1] + a2[2]
+        for i in range(3):
+            second(i, 1).wait_recv()
+        done[hd:DZ] = sb[y] + b2[0] + b2[1] + b2[2]
+
+        @pl.when(ex != z)
+        def _():
+            remote(done, back, ks.at[0], kr.at[0], swap).start()
+
+        @pl.when(ex == z)
+        def _():
+            back[...] = done[...]
+
+    def finish(e):
+        away(e).wait_recv()
+        ours = wgot[1, e]
+        theirs = wfar[e].astype(F32)
+        low = jnp.where(xh == 0, ours, theirs)
+        high = jnp.where(xh == 0, theirs, ours)
+        gate[e] = jnp.concatenate([low[:, 0:FH], high[:, 0:FH]], axis=1)
+        up_out[e] = jnp.concatenate([low[:, FH : 2 * FH], high[:, FH : 2 * FH]], axis=1)
+        down_out[e] = jnp.concatenate([low[:, 2 * FH : F3].T, high[:, 2 * FH : F3].T], axis=0)
 
     def per_expert(e, carry):
         weights(e)
@@ -390,58 +444,28 @@
         def _():
             combine(e - 1)
 
+        @pl.when(e == 0)
+        def _():
+            rows_second()
+
+        @pl.when(e == 3)
+        def _():
+            rows_swap()
+
+        @pl.when(e > 4)
+        def _():
+            finish(e - 5)
+
         return carry
 
     lax.fori_loop(0, EXPERTS, per_expert, 0)
     combine(EXPERTS - 1)
 
-    for i in range(3):
-        for j in range(NXH):
-            for k in range(NXL):
-                remote(
-                    dx.at[0, 0, 0, pl.ds(0, hd)], a1.at[i, j, k], a1s.at[0, 0], a1r.at[i, j, k], up
-                ).wait_recv()
-    for j in range(NXH):
-        for k in range(NXL):
-            sa[j, k] = dx[j, k, y, 0:hd] + a1[0, j, k] + a1[1, j, k] + a1[2, j, k]
-    ca2 = []
-    for i in range(3):
-        t = (pos + i + 1) % 4
-        ca2.append(remote(sa.at[t // 2, t % 2], a2.at[i], a2s.at[i], a2r.at[i], xp[i]))
-        ca2[-1].start()
-    for i in range(3):
-        for j in range(NY):
-            remote(
-                dx.at[0, 0, 0, pl.ds(hd, hd)], b1.at[i, j], b1s.at[0, 0], b1r.at[i, j], up
-            ).wait_recv()
-    for j in range(NY):
-        sb[j] = dx[xh, xl, j, hd:DZ] + b1[0, j] + b1[1, j] + b1[2, j]
-    cb2 = []
-    for i in range(3):
-        t = (y + i + 1) % NY
-        cb2.append(remote(sb.at[t], b2.at[i], b2s.at[i], b2r.at[i], yp[i]))
-        cb2[-1].start()
-    for k in ca2:
-        k.wait_recv()
-    done[0:hd] = sa[xh, xl] + a2[0] + a2[1] + a2[2]
-    for k in cb2:
-        k.wait_recv()
-    done[hd:DZ] = sb[y] + b2[0] + b2[1] + b2[2]
-
-    @pl.when(ex != z)
-    def _():
-        remote(done, xout, ks.at[0], kr.at[0], swap).start()
-
-    @pl.when(ex == z)
-    def _():
-        xout[...] = done[...]
-
-    def widen(e, carry):
-        away(e).wait_recv()
-        wout[1 - xh, e] = wfar[e].astype(F32)
+    def finish_rest(e, carry):
+        finish(e)
         return carry
 
-    lax.fori_loop(0, EXPERTS, widen, 0)
+    lax.fori_loop(EXPERTS - 5, EXPERTS, finish_rest, 0)
 
     def drain_ring(s, carry):
         for half in range(2):
@@ -456,9 +480,9 @@
             gather(half, slot, 0, z).wait_send()
 
     def drain(s, carry):
+        for i in range(3):
+            spread(s, i).wait_send()
         for half in range(2):
-            for i in range(3):
-                spread(half, s, i).wait_send()
             for i, make in (rows_a(half, s), rows_b(half, s)):
 
                 @pl.when(i != 0)
@@ -471,12 +495,15 @@
         return carry
 
     lax.fori_loop(0, NZ, drain, 0)
-    for k in ca2 + cb2:
-        k.wait_send()
+    for i in range(3):
+        second(i, 0).wait_send()
+        second(i, 1).wait_send()
 
     @pl.when(ex != z)
     def _():
-        remote(done, xout, ks.at[0], kr.at[0], swap).wait()
+        remote(done, back, ks.at[0], kr.at[0], swap).wait()
+
+    xout[...] = back[...].T
 
 
 def layer(ids, xin, w, wt, scale):
@@ -488,17 +515,17 @@
     return pl.pallas_call(
         layer_kernel,
         out_shape=(
-            jax.ShapeDtypeStruct((NXH, EXPERTS, SUB, FP), F32),
-            jax.ShapeDtypeStruct((DZ, TOK), F32),
+            jax.ShapeDtypeStruct((EXPERTS, SUB, 2 * FH), F32),
+            jax.ShapeDtypeStruct((EXPERTS, SUB, 2 * FH), F32),
+            jax.ShapeDtypeStruct((EXPERTS, 2 * FH, SUB), F32),
+            jax.ShapeDtypeStruct((TOK, DZ), F32),
         ),
         in_specs=[pl.BlockSpec(memory_space=pltpu.SMEM), vm, vm, vm, vm],
-        out_specs=(vm, vm),
+        out_specs=(vm,) * 4,
         scratch_shapes=[
-            pltpu.VMEM((NXH, NXL, NY, NZ, SUB, TOK), BF16),
+            pltpu.VMEM((2, DZ, cols), BF16),
             pltpu.VMEM((2, NZ - 1, SLOTS, F3, TOK), F32),
             pltpu.VMEM((2, SLOTS, F3, TOK), F32),
-            pltpu.VMEM((NZ, NXH, SLOTS, FP, TOK), BF16),
-            pltpu.VMEM((DZ, cols), BF16),
             pltpu.VMEM((SLOTS, DZ, cols), BF16),
             pltpu.VMEM((SLOTS, FP, cols), BF16),
             pltpu.VMEM((NXH, NXL, NY, DZ, TOK), F32),
@@ -513,9 +540,9 @@
             pltpu.VMEM((NXH, NXL, hd, TOK), F32),
             pltpu.VMEM((NY, hd, TOK), F32),
             pltpu.VMEM((DZ, TOK), F32),
-            dma((1,)),
-            dma((2, NZ, 3)),
-            dma((2, NZ, 3)),
+            pltpu.VMEM((DZ, TOK), F32),
+            dma((NZ, 3)),
+            dma((NZ, 3)),
         ]
         + [dma((2, NZ - 1, SLOTS))] * 4
         + [dma((2, NZ)), dma((3, NXH, NXL)), dma((2, NZ)), dma((3, NY))]
@@ -570,15 +597,10 @@
 
     xin, info_all, w_all, wt = exchange(piece, info, wsend)
     ids = info_all[:, :, 2:4, 0].astype(jnp.int32).reshape(-1)
-    wout, xout = layer(ids, xin, w_all.reshape(EXPERTS, DZ, FP), wt, info_all)
-    grad_gate = jnp.concatenate([wout[0, :, :, 0:FH], wout[1, :, :, 0:FH]], axis=2)
-    grad_up = jnp.concatenate(
-        [wout[0, :, :, FH : 2 * FH], wout[1, :, :, FH : 2 * FH]], axis=2
+    grad_gate, grad_up, grad_down, rows = layer(
+        ids, xin, w_all.reshape(EXPERTS, DZ, FP), wt, info_all
     )
-    grad_down = jnp.concatenate(
-        [wout[0, :, :, 2 * FH : F3], wout[1, :, :, 2 * FH : F3]], axis=2
-    ).transpose(0, 2, 1)
-    return xout.T, grad_gate, grad_up, grad_down
+    return rows, grad_gate, grad_up, grad_down
 
 
 def solution(mesh):

time: 260 us -> 239 us (0.919)
  the two profiles are of different devices: /device:TPU:64 before, /device:TPU:4 now
where the time goes in v3:
time: 239 us
  Pallas kernels  217 us (91%)
  local copies, waits for them, and re-layouts  13.5 us (6%)
  other arithmetic  7.16 us (3%)
    pallas_call x1, Pallas kernels, layer(): pl.pallas_call(layer_kernel, out_shape=(jax.ShapeDtypeStruct((EXPERTS, SU...  182 us
    pallas_call x1, Pallas kernels, exchange(): pl.pallas_call(exchange_kernel, out_shape=(jax.ShapeDtypeStruct((NZ, DZ,...  35.4 us
    unnamed x23, local copies, waits for them, and re-layouts  10.6 us

profile of v3, /device:TPU:4, one launch (start us, length us, event | category | flops | bytes accessed | tf_op | source)
XLA Modules:
  0.0 238.6 jit_solution(14831312597154845499)
XLA Ops:
  0.6 0.0 copy-start.5
  0.7 0.7 convert_bitcast_fusion
  1.4 0.1 pad.11.clone
  1.5 0.1 pad.12.clone
  1.5 0.1 pad.9.clone
  1.6 0.8 compare_select_fusion
  2.4 0.8 select_reduce_fusion
  3.2 0.7 maximum_maximum_fusion.info
  3.9 1.1 fusion.1
  5.0 0.2 copy.42
  5.2 0.0 copy-start.4
  5.2 0.2 copy.44
  5.4 0.0 copy-done.5
  5.5 0.2 copy.43
  5.7 0.2 copy.45
  5.9 0.4 copy-done.4
  6.3 0.3 copy.36
  6.6 0.2 fusion
  6.8 1.4 maximum_bitcast_fusion
  8.2 0.0 copy-start.2
  8.2 1.5 pad_maximum_fusion.wsend
  9.8 0.0 copy-done.2
  9.8 0.0 copy-start.3
  9.8 0.6 copy.32
  10.4 0.6 copy-done.3
  11.0 0.6 copy.33
  11.6 0.1 broadcast_select_fusion
  11.7 0.7 dynamic-slice_bitcast_fusion.piece
  12.4 35.4 %exchange_in.1 = (bf16[8,448,128]{2,1,0:T(8,128)(2,1)}, f32[2,8,8,128]{3,2,1,0:T(8,128)}, bf16[8,4,112,464]{3,2,1,0:T(8,128)(2,1)}, bf16[8,464,448]{2,1,0:T(8,128)(2,1)}) custom-call(bf16[8,112,128]{2,1,0:T(8,128)(2,1)} %dynamic-slice_bitcast_fusion.piece, f32[8,128]{1,0:T(8,128)} %maximum_maximum_fusion.info, bf16[2,8,112,464]{3,2,1,0:T(8,128)(2,1)} %pad_maximum_fusion.wsend), custom_call_target="tpu_custom_call" | custom-call | tf_op jit(solution)/shard_map/exchange_in/pallas_call | solution.py:138
  47.8 1.2 convert_reduce_fusion
  49.0 0.6 convert_element_type.20.ids
  49.6 181.8 %layer.1 = (f32[8,112,304]{2,1,0:T(8,128)}, f32[8,112,304]{2,1,0:T(8,128)}, f32[8,304,112]{2,1,0:T(8,128)}, f32[128,448]{1,0:T(8,128)}) custom-call(s32[32]{0:T(128)} %convert_element_type.20.ids, bf16[8,448,128]{2,1,0:T(8,128)(2,1)} %get-tuple-element.13.xin, bf16[8,448,464]{2,1,0:T(8,128)(2,1)} %bitcast.18, bf16[8,464,448]{2,1,0:T(8,128)(2,1)} %get-tuple-element.15.wt, ...), custom_call_target="tpu_custom_call" | custom-call | tf_op jit(solution)/shard_map/layer/pallas_call | solution.py:515
  231.4 0.0 copy-start
  231.4 1.9 copy.39
  233.3 2.8 %copy.40 = f32[8,112,304]{1,2,0:T(8,128)} copy(f32[8,112,304]{2,1,0:T(8,128)} %get-tuple-element.29) | data formatting | bytes 2179072
  236.1 0.0 copy-done
  236.1 0.0 copy-start.1
  236.1 1.5 copy.41
  237.6 0.0 copy-done.1
  237.6 1.0 copy.47
  (3 shorter events, 0.1 us)
Async XLA Ops:
  0.6 4.8 %copy-start.5 = (bf16[8,112,304]{1,2,0:T(8,128)(2,1)S(1)}, bf16[8,112,304]{1,2,0:T(8,128)(2,1)}, u32[]{:S(2)}) copy-start(bf16[8,112,304]{1,2,0:T(8,128)(2,1)} %param.16) | copy-start | bytes 1634308
  5.2 1.1 copy-start.4
  8.2 1.5 copy-start.2
  9.8 1.2 copy-start.3
  231.4 4.7 %copy-start = (f32[8,112,304]{2,1,0:T(8,128)S(1)}, f32[8,112,304]{2,1,0:T(8,128)}, u32[]{:S(2)}) copy-start(f32[8,112,304]{2,1,0:T(8,128)} %get-tuple-element.30) | copy-start | bytes 3268612
  236.1 1.5 copy-start.1

commit v4 on v3

--- a/solution.py
+++ b/solution.py
@@ -18,6 +18,7 @@
 FH = 152
 F3 = 3 * FH
 FP = 464
+NB = 3
 VMEM_LIMIT = 58 * 1024 * 1024
 
 
@@ -156,7 +157,7 @@
 
 def layer_kernel(
     ids, xin, w, wt, scale, gate, up_out, down_out, xout,
-    x, acc, own, dcat, hcat, dx, dw, wgot, wsnd, wfar, a1, a2, b1, b2, sa, sb, done, back,
+    x, early, first, acc, turn, own, dcat, hcat, dx, dxs, dw, wgot, wsnd, wfar, a1, a2, b1, b2, sa, sb, done, mid, back,
     x_s, x_r, rs_s, rs_r, ag_s, ag_r,
     a1s, a1r, b1s, b1r, a2s, a2r, b2s, b2r, ts, tr, fs, fr, ks, kr,
 ):
@@ -170,16 +171,25 @@
     to = (up, down)
     far = device(xl, y, z, 1 - xh, c)
     twin = device(xl, y, z, xh, 1 - c)
-    swap = device(z // NY, z % NY, ex, xh, c)
+    pair = (ex + NZ - z) % NZ
+    along = device(xl, y, pair, xh, c)
+    across = device(pair // NY, pair % NY, z, xh, c)
+    before = (ex + z) % NZ
+    source = device(before // NY, before % NY, z, xh, c)
     barrier = pltpu.get_barrier_semaphore()
     for dev in xp + yp + [up, down, twin]:
         pl.semaphore_signal(barrier, inc=1, device_id=dev, device_id_type=MESH)
 
-    @pl.when(ex != z)
+    @pl.when(pair != z)
     def _():
-        pl.semaphore_signal(barrier, inc=1, device_id=swap, device_id_type=MESH)
-
-    pl.semaphore_wait(barrier, 9 + jnp.where(ex != z, 1, 0))
+        pl.semaphore_signal(barrier, inc=1, device_id=along, device_id_type=MESH)
+
+    @pl.when(z != 0)
+    def _():
+        pl.semaphore_signal(barrier, inc=1, device_id=across, device_id_type=MESH)
+        pl.semaphore_signal(barrier, inc=1, device_id=source, device_id_type=MESH)
+
+    pl.semaphore_wait(barrier, 9 + jnp.where(pair != z, 1, 0) + jnp.where(z != 0, 2, 0))
 
     def lanes(half, gz):
         return pl.ds(pl.multiple_of((half * NZ + gz) * TOK, TOK), TOK)
@@ -217,36 +227,61 @@
             gu = jnp.dot(wt[e, 0 : 2 * FH, :], xt, preferred_element_type=F32)
             dh = jnp.dot(wt[e, 2 * FH : FP, :], dys, preferred_element_type=F32)
             own[half, slot, 0 : 2 * FH, :] = gu
-            own[half, slot, 2 * FH : F3, :] = dh[:FH]
-
-    def hop(half, slot, s, src):
-        return remote(
-            src, acc.at[half, s, slot], rs_s.at[half, s, slot], rs_r.at[half, s, slot], to[half]
-        )
+            own[half, slot, 2 * FH : FP, :] = dh
+
+    def hop(half, slot, s, src, dst):
+        return remote(src, dst, rs_s.at[half, s, slot], rs_r.at[half, s, slot], to[half])
+
+    def hop16(half, slot, s, src):
+        return hop(half, slot, s, src, early.at[half, s, slot])
+
+    def hop32(half, slot, s, src):
+        return hop(half, slot, s, src, acc.at[half, s - NB, slot])
 
     await_all(0)
     for half in range(2):
         partial(half, chunk(half, 0))
         for slot in range(SLOTS):
-            hop(half, slot, 0, own.at[half, slot]).start()
-    for half in range(2):
-        for slot in range(SLOTS):
-            hop(half, slot, 0, own.at[half, slot]).wait_send()
-
-    def ring(s, carry):
+            first[half, slot] = own[half, slot].astype(BF16)
+            hop16(half, slot, 0, first.at[half, slot]).start()
+
+    def fresh(s):
         spread_all(s + 1)
         await_all(s)
         for half in range(2):
             partial(half, chunk(half, s))
+
+    def ring16(s, carry):
+        fresh(s)
         for slot in range(SLOTS):
             for half in range(2):
-                here = acc.at[half, s - 1, slot]
-                hop(half, slot, s - 1, here).wait_recv()
-                acc[half, s - 1, slot] = acc[half, s - 1, slot] + own[half, slot]
-                hop(half, slot, s, here).start()
+                here = early.at[half, s - 1, slot]
+                hop16(half, slot, s - 1, here).wait_recv()
+                total = early[half, s - 1, slot].astype(F32) + own[half, slot]
+                early[half, s - 1, slot] = total.astype(BF16)
+                hop16(half, slot, s, here).start()
         return carry
 
-    lax.fori_loop(1, NZ - 1, ring, 0)
+    lax.fori_loop(1, NB, ring16, 0)
+    fresh(NB)
+    for slot in range(SLOTS):
+        for half in range(2):
+            here = early.at[half, NB - 1, slot]
+            hop16(half, slot, NB - 1, here).wait_recv()
+            turn[half, slot] = early[half, NB - 1, slot, 0:F3].astype(F32) + own[half, slot, 0:F3]
+            hop32(half, slot, NB, turn.at[half, slot]).start()
+
+    def ring32(s, carry):
+        fresh(s)
+        for slot in range(SLOTS):
+            for half in range(2):
+                here = acc.at[half, s - 1 - NB, slot]
+                hop32(half, slot, s - 1, here).wait_recv()
+                acc[half, s - 1 - NB, slot] = acc[half, s - 1 - NB, slot] + own[half, slot, 0:F3]
+                hop32(half, slot, s, here).start()
+        return carry
+
+    lax.fori_loop(NB + 1, NZ - 1, ring32, 0)
     await_all(NZ - 1)
 
     def gather(half, slot, s, gz):
@@ -256,20 +291,25 @@
     def origin(half, s):
         return (z + NZ - s) % NZ if half == 0 else (z + s) % NZ
 
+    def spot(gz):
+        return (gz + z) % NZ
+
     def rows_a(half, gz):
-        i = (gz % NY - y + NY) % NY
-        src = dx.at[half, gz // NY, gz % NY, pl.ds(0, hd)]
+        q = spot(gz)
+        i = (q % NY - y + NY) % NY
+        src = dxs.at[half, q // NY, q % NY, pl.ds(0, hd)]
         return i, lambda: remote(
-            src, a1.at[i - 1, half, gz // NY], a1s.at[half, gz], a1r.at[i - 1, half, gz // NY],
-            device(xl, gz % NY, z, xh, c),
+            src, a1.at[i - 1, half, q // NY], a1s.at[half, gz], a1r.at[i - 1, half, q // NY],
+            device(xl, q % NY, z, xh, c),
         )
 
     def rows_b(half, gz):
-        i = (half * 2 + gz // NY - pos + 4) % 4
-        src = dx.at[half, gz // NY, gz % NY, pl.ds(hd, hd)]
+        q = spot(gz)
+        i = (half * 2 + q // NY - pos + 4) % 4
+        src = dxs.at[half, q // NY, q % NY, pl.ds(hd, hd)]
         return i, lambda: remote(
-            src, b1.at[i - 1, gz % NY], b1s.at[half, gz], b1r.at[i - 1, gz % NY],
-            device(gz // NY, y, z, half, c),
+            src, b1.at[i - 1, q % NY], b1s.at[half, gz], b1r.at[i - 1, q % NY],
+            device(q // NY, y, z, half, c),
         )
 
     def rows(half, gz):
@@ -280,7 +320,9 @@
             total = total + jnp.dot(
                 w[e, :, 0 : 2 * FH], hs, preferred_element_type=F32
             )
-        dx[half, gz // NY, gz % NY] = total
+        q = spot(gz)
+        dx[half, q // NY, q % NY] = total
+        dxs[half, q // NY, q % NY] = total.astype(BF16)
         for i, make in (rows_a(half, gz), rows_b(half, gz)):
 
             @pl.when(i != 0)
@@ -291,11 +333,11 @@
         partial(half, z)
     for slot in range(SLOTS):
         for half in range(2):
-            last = acc.at[half, NZ - 2, slot]
-            hop(half, slot, NZ - 2, last).wait_recv()
-            g = acc[half, NZ - 2, slot, 0:FH, :] + own[half, slot, 0:FH, :]
-            u = acc[half, NZ - 2, slot, FH : 2 * FH, :] + own[half, slot, FH : 2 * FH, :]
-            dh = acc[half, NZ - 2, slot, 2 * FH : F3, :] + own[half, slot, 2 * FH : F3, :]
+            last = acc.at[half, NZ - 2 - NB, slot]
+            hop32(half, slot, NZ - 2, last).wait_recv()
+            g = acc[half, NZ - 2 - NB, slot, 0:FH, :] + own[half, slot, 0:FH, :]
+            u = acc[half, NZ - 2 - NB, slot, FH : 2 * FH, :] + own[half, slot, FH : 2 * FH, :]
+            dh = acc[half, NZ - 2 - NB, slot, 2 * FH : F3, :] + own[half, slot, 2 * FH : F3, :]
             sig = 1.0 / (1.0 + jnp.exp(-g))
             act = g * sig
             dg = dh * u * sig * (1.0 + g * (1.0 - sig))
@@ -391,21 +433,25 @@
             for j in range(NXH):
                 for k in range(NXL):
                     remote(
-                        dx.at[0, 0, 0, pl.ds(0, hd)], a1.at[i, j, k], a1s.at[0, 0],
+                        dxs.at[0, 0, 0, pl.ds(0, hd)], a1.at[i, j, k], a1s.at[0, 0],
                         a1r.at[i, j, k], up,
                     ).wait_recv()
         for j in range(NXH):
             for k in range(NXL):
-                sa[j, k] = dx[j, k, y, 0:hd] + a1[0, j, k] + a1[1, j, k] + a1[2, j, k]
+                sa[j, k] = dx[j, k, y, 0:hd] + (
+                    a1[0, j, k].astype(F32) + a1[1, j, k].astype(F32) + a1[2, j, k].astype(F32)
+                )
         for i in range(3):
             second(i, 0).start()
         for i in range(3):
             for j in range(NY):
                 remote(
-                    dx.at[0, 0, 0, pl.ds(hd, hd)], b1.at[i, j], b1s.at[0, 0], b1r.at[i, j], up
+                    dxs.at[0, 0, 0, pl.ds(hd, hd)], b1.at[i, j], b1s.at[0, 0], b1r.at[i, j], up
                 ).wait_recv()
         for j in range(NY):
-            sb[j] = dx[xh, xl, j, hd:DZ] + b1[0, j] + b1[1, j] + b1[2, j]
+            sb[j] = dx[xh, xl, j, hd:DZ] + (
+                b1[0, j].astype(F32) + b1[1, j].astype(F32) + b1[2, j].astype(F32)
+            )
         for i in range(3):
             second(i, 1).start()
 
@@ -417,13 +463,32 @@
             second(i, 1).wait_recv()
         done[hd:DZ] = sb[y] + b2[0] + b2[1] + b2[2]
 
-        @pl.when(ex != z)
-        def _():
-            remote(done, back, ks.at[0], kr.at[0], swap).start()
-
-        @pl.when(ex == z)
-        def _():
-            back[...] = done[...]
+        @pl.when(pair != z)
+        def _():
+            first_step().start()
+
+    def first_step():
+        return remote(done, mid, ks.at[0], kr.at[0], along)
+
+    def second_step():
+        return remote(mid, back, ks.at[1], kr.at[1], across)
+
+    def rows_turn():
+        @pl.when(pair != z)
+        def _():
+            first_step().wait_recv()
+
+        @pl.when(pair == z)
+        def _():
+            mid[...] = done[...]
+
+        @pl.when(z != 0)
+        def _():
+            second_step().start()
+
+        @pl.when(z == 0)
+        def _():
+            back[...] = mid[...]
 
     def finish(e):
         away(e).wait_recv()
@@ -448,9 +513,13 @@
         def _():
             rows_second()
 
-        @pl.when(e == 3)
+        @pl.when(e == 2)
         def _():
             rows_swap()
+
+        @pl.when(e == 5)
+        def _():
+            rows_turn()
 
         @pl.when(e > 4)
         def _():
@@ -470,10 +539,17 @@
     def drain_ring(s, carry):
         for half in range(2):
             for slot in range(SLOTS):
-                hop(half, slot, s, acc.at[half, s - 1, slot]).wait_send()
                 gather(half, slot, s, origin(half, s)).wait_send()
         return carry
 
+    for half in range(2):
+        for slot in range(SLOTS):
+            hop16(half, slot, 0, first.at[half, slot]).wait_send()
+            for s in range(1, NB):
+                hop16(half, slot, s, early.at[half, s - 1, slot]).wait_send()
+            hop32(half, slot, NB, turn.at[half, slot]).wait_send()
+            for s in range(NB + 1, NZ - 1):
+                hop32(half, slot, s, acc.at[half, s - 1 - NB, slot]).wait_send()
     lax.fori_loop(1, NZ - 1, drain_ring, 0)
     for half in range(2):
         for slot in range(SLOTS):
@@ -499,9 +575,13 @@
         second(i, 0).wait_send()
         second(i, 1).wait_send()
 
-    @pl.when(ex != z)
+    @pl.when(pair != z)
     def _():
-        remote(done, back, ks.at[0], kr.at[0], swap).wait()
+        first_step().wait_send()
+
+    @pl.when(z != 0)
+    def _():
+        second_step().wait()
 
     xout[...] = back[...].T
 
@@ -524,21 +604,26 @@
         out_specs=(vm,) * 4,
         scratch_shapes=[
             pltpu.VMEM((2, DZ, cols), BF16),
-            pltpu.VMEM((2, NZ - 1, SLOTS, F3, TOK), F32),
+            pltpu.VMEM((2, NB, SLOTS, FP, TOK), BF16),
+            pltpu.VMEM((2, SLOTS, FP, TOK), BF16),
+            pltpu.VMEM((2, NZ - 1 - NB, SLOTS, F3, TOK), F32),
             pltpu.VMEM((2, SLOTS, F3, TOK), F32),
+            pltpu.VMEM((2, SLOTS, FP, TOK), F32),
             pltpu.VMEM((SLOTS, DZ, cols), BF16),
             pltpu.VMEM((SLOTS, FP, cols), BF16),
             pltpu.VMEM((NXH, NXL, NY, DZ, TOK), F32),
+            pltpu.VMEM((NXH, NXL, NY, DZ, TOK), BF16),
             pltpu.VMEM((EXPERTS, NXH * NC, SUB, FP), F32),
             pltpu.VMEM((2,) + block, F32),
             pltpu.VMEM(block, BF16),
             pltpu.VMEM(block, BF16),
-            pltpu.VMEM((3, NXH, NXL, hd, TOK), F32),
+            pltpu.VMEM((3, NXH, NXL, hd, TOK), BF16),
             pltpu.VMEM((3, hd, TOK), F32),
-            pltpu.VMEM((3, NY, hd, TOK), F32),
+            pltpu.VMEM((3, NY, hd, TOK), BF16),
             pltpu.VMEM((3, hd, TOK), F32),
             pltpu.VMEM((NXH, NXL, hd, TOK), F32),
             pltpu.VMEM((NY, hd, TOK), F32),
+            pltpu.VMEM((DZ, TOK), F32),
             pltpu.VMEM((DZ, TOK), F32),
             pltpu.VMEM((DZ, TOK), F32),
             dma((NZ, 3)),
@@ -549,7 +634,7 @@
         + [dma((3,))] * 4
         + [dma((2, EXPERTS))] * 2
         + [dma((EXPERTS,))] * 2
-        + [dma((1,))] * 2,
+        + [dma((2,))] * 2,
         compiler_params=pltpu.CompilerParams(
             collective_id=1, has_side_effects=True, vmem_limit_bytes=VMEM_LIMIT
         ),

time: 239 us -> 218 us (0.912)
  the two profiles are of different devices: /device:TPU:4 before, /device:TPU:72 now
where the time goes in v4:
time: 218 us; the launch traced here: 215 us
  Pallas kernels  194 us (89%)
  local copies, waits for them, and re-layouts  13.5 us (6%)
  other arithmetic  7.16 us (3%)
    pallas_call x1, Pallas kernels, layer(): pl.pallas_call(layer_kernel, out_shape=(jax.ShapeDtypeStruct((EXPERTS, SU...  158 us
    pallas_call x1, Pallas kernels, exchange(): pl.pallas_call(exchange_kernel, out_shape=(jax.ShapeDtypeStruct((NZ, DZ,...  36.1 us
    unnamed x23, local copies, waits for them, and re-layouts  10.6 us

profile of v4, /device:TPU:72, one launch (start us, length us, event | category | flops | bytes accessed | tf_op | source)
XLA Modules:
  0.0 215.4 jit_solution(11246686836758279626)
XLA Ops:
  0.6 0.0 copy-start.5
  0.7 0.7 convert_bitcast_fusion
  1.4 0.1 pad.11.clone
  1.5 0.1 pad.12.clone
  1.5 0.1 pad.9.clone
  1.6 0.8 compare_select_fusion
  2.4 0.8 select_reduce_fusion
  3.2 0.7 maximum_maximum_fusion.info
  3.9 1.1 fusion.1
  5.0 0.2 copy.42
  5.2 0.0 copy-start.4
  5.2 0.2 copy.44
  5.4 0.0 copy-done.5
  5.5 0.2 copy.43
  5.7 0.2 copy.45
  5.9 0.4 copy-done.4
  6.3 0.3 copy.36
  6.6 0.2 fusion
  6.8 1.4 maximum_bitcast_fusion
  8.2 0.0 copy-start.2
  8.2 1.5 pad_maximum_fusion.wsend
  9.8 0.0 copy-done.2
  9.8 0.0 copy-start.3
  9.8 0.6 copy.32
  10.4 0.6 copy-done.3
  11.0 0.6 copy.33
  11.6 0.1 broadcast_select_fusion
  11.7 0.7 dynamic-slice_bitcast_fusion.piece
  12.4 36.1 %exchange_in.1 = (bf16[8,448,128]{2,1,0:T(8,128)(2,1)}, f32[2,8,8,128]{3,2,1,0:T(8,128)}, bf16[8,4,112,464]{3,2,1,0:T(8,128)(2,1)}, bf16[8,464,448]{2,1,0:T(8,128)(2,1)}) custom-call(bf16[8,112,128]{2,1,0:T(8,128)(2,1)} %dynamic-slice_bitcast_fusion.piece, f32[8,128]{1,0:T(8,128)} %maximum_maximum_fusion.info, bf16[2,8,112,464]{3,2,1,0:T(8,128)(2,1)} %pad_maximum_fusion.wsend), custom_call_target="tpu_custom_call" | custom-call | tf_op jit(solution)/shard_map/exchange_in/pallas_call | solution.py:139
  48.5 1.2 convert_reduce_fusion
  49.7 0.6 convert_element_type.20.ids
  50.3 157.9 %layer.1 = (f32[8,112,304]{2,1,0:T(8,128)}, f32[8,112,304]{2,1,0:T(8,128)}, f32[8,304,112]{2,1,0:T(8,128)}, f32[128,448]{1,0:T(8,128)}) custom-call(s32[32]{0:T(128)} %convert_element_type.20.ids, bf16[8,448,128]{2,1,0:T(8,128)(2,1)} %get-tuple-element.13.xin, bf16[8,448,464]{2,1,0:T(8,128)(2,1)} %bitcast.18, bf16[8,464,448]{2,1,0:T(8,128)(2,1)} %get-tuple-element.15.wt, ...), custom_call_target="tpu_custom_call" | custom-call | tf_op jit(solution)/shard_map/layer/pallas_call | solution.py:595
  208.2 0.0 copy-start
  208.2 1.9 copy.39
  210.1 2.8 %copy.40 = f32[8,112,304]{1,2,0:T(8,128)} copy(f32[8,112,304]{2,1,0:T(8,128)} %get-tuple-element.29) | data formatting | bytes 2179072
  212.9 0.0 copy-done
  212.9 0.0 copy-start.1
  212.9 1.5 copy.41
  214.4 0.0 copy-done.1
  214.4 1.0 copy.47
  (3 shorter events, 0.1 us)
Async XLA Ops:
  0.6 4.8 %copy-start.5 = (bf16[8,112,304]{1,2,0:T(8,128)(2,1)S(1)}, bf16[8,112,304]{1,2,0:T(8,128)(2,1)}, u32[]{:S(2)}) copy-start(bf16[8,112,304]{1,2,0:T(8,128)(2,1)} %param.16) | copy-start | bytes 1634308
  5.2 1.1 copy-start.4
  8.2 1.5 copy-start.2
  9.8 1.2 copy-start.3
  208.2 4.7 %copy-start = (f32[8,112,304]{2,1,0:T(8,128)S(1)}, f32[8,112,304]{2,1,0:T(8,128)}, u32[]{:S(2)}) copy-start(f32[8,112,304]{2,1,0:T(8,128)} %get-tuple-element.30) | copy-start | bytes 3268612
  212.9 1.5 copy-start.1

commit v5 on v4

--- a/solution.py
+++ b/solution.py
@@ -19,6 +19,8 @@
 F3 = 3 * FH
 FP = 464
 NB = 3
+SWAP_AT = 7
+TURN_AT = 4
 VMEM_LIMIT = 58 * 1024 * 1024
 
 
@@ -63,43 +65,86 @@
 
 
 def exchange_kernel(
-    piece, info, wsend, x_out, info_out, w_out, wt_out,
+    act, cot, rows, counts, probs, ids, wg, wu, wd, x_out, info_out, w_all, wt_out,
+    xt, stack, info, wsrc,
     zs, zr, is_, ir, ys, yr, ixs, ixr, fs, fr, os_, or_, ps, pr, loc,
 ):
     xl, y, z, xh, c = me = place()
     zp, yp = z_peers(*me), y_peers(*me)
     far = device(xl, y, z, 1 - xh, c)
     twin = device(xl, y, z, xh, 1 - c)
-    greet(zp + yp + [far, twin])
     part = pl.ds(pl.multiple_of(y * SUB, SUB), SUB)
     mine = 2 * xh + c
     other = 2 * (1 - xh) + c
+    barrier = pltpu.get_barrier_semaphore()
+    peers = zp + yp + [far, twin]
+    for dev in peers:
+        pl.semaphore_signal(barrier, inc=1, device_id=dev, device_id_type=MESH)
+
+    def pack(e, carry):
+        g = wg[e].astype(F32)
+        u = wu[e].astype(F32)
+        d = wd[e].astype(F32).T
+        both = []
+        for i in range(NXH):
+            pieces = [v[:, i * FH : (i + 1) * FH] for v in (g, u, d)]
+            pieces.append(jnp.zeros((SUB, FP - F3), F32))
+            both.append(jnp.concatenate(pieces, axis=1))
+        wsrc[e] = jnp.where(xh == 0, both[1], both[0]).astype(BF16)
+        w_all[e, mine] = jnp.where(xh == 0, both[0], both[1]).astype(BF16)
+        return carry
+
+    lax.fori_loop(0, EXPERTS, pack, 0)
+    pl.semaphore_wait(barrier, len(peers))
 
     wfar = []
     for e in range(EXPERTS):
-        wfar.append(
-            remote(wsend.at[1 - xh, e], w_out.at[e, mine], fs.at[e], fr.at[e], far)
-        )
+        wfar.append(remote(wsrc.at[e], w_all.at[e, mine], fs.at[e], fr.at[e], far))
         wfar[-1].start()
+    wown = []
+    for e in range(EXPERTS):
+        wown.append(remote(w_all.at[e, mine], w_all.at[e, mine], os_.at[e], or_.at[e], twin))
+        wown[-1].start()
+
+    def turn_rows(j, carry):
+        cols = pl.ds(pl.multiple_of(j * TOK, TOK), TOK)
+        xt[cols, :] = jnp.where(xl == 0, act[:, cols], cot[:, cols]).T
+        return carry
+
+    lax.fori_loop(0, NZ * DZ // TOK, turn_rows, 0)
+
+    def piece(gz):
+        return xt.at[pl.ds(pl.multiple_of(gz * DZ + y * SUB, 16), SUB)]
+
     cz = []
     for i in range(NZ - 1):
         to = (z + i + 1) % NZ
-        cz.append(remote(piece.at[to], x_out.at[z, part], zs.at[i], zr.at[i], zp[i]))
+        cz.append(remote(piece(to), x_out.at[z, part], zs.at[i], zr.at[i], zp[i]))
         cz[-1].start()
+
+    lane = lax.broadcasted_iota(jnp.int32, (1, TOK), 1)
+    column = lax.broadcasted_iota(jnp.int32, (TOK, TOK), 1).astype(F32)
+    for slot in range(SLOTS):
+        stack[slot : slot + 1, :] = rows[slot : slot + 1, :].astype(F32)
+        stack[2 + slot : 3 + slot, :] = jnp.where(
+            lane < counts[0, slot], probs[slot : slot + 1, :], 0.0
+        )
+    stack[4:8, :] = jnp.zeros((4, TOK), F32)
+    turned = stack[...].T
+    info[4:8, :] = jnp.zeros((4, TOK), F32)
+    for slot in range(SLOTS):
+        hit = turned[:, slot : slot + 1] == column
+        info[slot : slot + 1, :] = jnp.sum(
+            jnp.where(hit, turned[:, 2 + slot : 3 + slot], 0.0), axis=0, keepdims=True
+        )
+        info[2 + slot : 3 + slot, :] = jnp.full((1, TOK), ids[0, slot], jnp.int32).astype(F32)
     ci = []
     for i in range(NZ - 1):
         ci.append(remote(info, info_out.at[xh, z], is_.at[i], ir.at[i], zp[i]))
         ci[-1].start()
-    wown = []
-    for e in range(EXPERTS):
-        wown.append(
-            remote(wsend.at[xh, e], w_out.at[e, mine], os_.at[e], or_.at[e], twin)
-        )
-        wown[-1].start()
     here = [
-        pltpu.make_async_copy(piece.at[z], x_out.at[z, part], loc.at[0]),
+        pltpu.make_async_copy(piece(z), x_out.at[z, part], loc.at[0]),
         pltpu.make_async_copy(info, info_out.at[xh, z], loc.at[1]),
-        pltpu.make_async_copy(wsend.at[xh], w_out.at[:, mine], loc.at[2]),
     ]
     for h in here:
         h.start()
@@ -119,13 +164,13 @@
     for e in range(EXPERTS):
         wfar[e].wait_recv()
         wpass.append(
-            remote(w_out.at[e, other], w_out.at[e, other], ps.at[e], pr.at[e], twin)
+            remote(w_all.at[e, other], w_all.at[e, other], ps.at[e], pr.at[e], twin)
         )
         wpass[-1].start()
     for e in range(EXPERTS):
         wown[e].wait_recv()
         wpass[e].wait_recv()
-        wt_out[e] = w_out[e].reshape(DZ, FP).T
+        wt_out[e] = w_all[e].reshape(DZ, FP).T
     for k in cy:
         k.wait()
     cinf.wait()
@@ -133,9 +178,10 @@
         k.wait_send()
 
 
-def exchange(piece, info, wsend):
+def exchange(act, cot, rows, counts, probs, ids, wg, wu, wd):
     dma = pltpu.SemaphoreType.DMA
     vm = pl.BlockSpec(memory_space=pltpu.VMEM)
+    sm = pl.BlockSpec(memory_space=pltpu.SMEM)
     return pl.pallas_call(
         exchange_kernel,
         out_shape=(
@@ -144,15 +190,21 @@
             jax.ShapeDtypeStruct((EXPERTS, NXH * NC, SUB, FP), BF16),
             jax.ShapeDtypeStruct((EXPERTS, FP, DZ), BF16),
         ),
-        in_specs=[vm] * 3,
+        in_specs=[vm, vm, vm, sm, vm, sm, vm, vm, vm],
         out_specs=(vm,) * 4,
-        scratch_shapes=[dma((7,))] * 4 + [dma((3,))] * 2 + [dma((1,))] * 2 + [dma((EXPERTS,))] * 6
-        + [dma((3,))],
+        scratch_shapes=[
+            pltpu.VMEM((NZ * DZ, TOK), BF16),
+            pltpu.VMEM((8, TOK), F32),
+            pltpu.VMEM((8, TOK), F32),
+            pltpu.VMEM((EXPERTS, SUB, FP), BF16),
+        ]
+        + [dma((7,))] * 4 + [dma((3,))] * 2 + [dma((1,))] * 2 + [dma((EXPERTS,))] * 6
+        + [dma((2,))],
         compiler_params=pltpu.CompilerParams(
             collective_id=0, has_side_effects=True, vmem_limit_bytes=VMEM_LIMIT
         ),
         name="exchange_in",
-    )(piece, info, wsend)
+    )(act, cot, rows, counts, probs, ids, wg, wu, wd)
 
 
 def layer_kernel(
@@ -513,28 +565,25 @@
         def _():
             rows_second()
 
-        @pl.when(e == 2)
+        @pl.when(e == SWAP_AT)
         def _():
             rows_swap()
-
-        @pl.when(e == 5)
-        def _():
-            rows_turn()
-
-        @pl.when(e > 4)
-        def _():
-            finish(e - 5)
 
         return carry
 
     lax.fori_loop(0, EXPERTS, per_expert, 0)
     combine(EXPERTS - 1)
 
-    def finish_rest(e, carry):
+    def finish_all(e, carry):
         finish(e)
-        return carry
-
-    lax.fori_loop(EXPERTS - 5, EXPERTS, finish_rest, 0)
+
+        @pl.when(e == TURN_AT)
+        def _():
+            rows_turn()
+
+        return carry
+
+    lax.fori_loop(0, EXPERTS, finish_all, 0)
 
     def drain_ring(s, carry):
         for half in range(2):
@@ -645,42 +694,10 @@
 def shards(
     activations, cotangent, expert_ids, slot_rows, slot_counts, route_probs, w_gate, w_up, w_down
 ):
-    ex = lax.axis_index("expert")
-    dp = lax.axis_index("dp")
-    xl, y, xh = ex // NY, ex % NY, (dp // 2) % 2
-
-    down_t = w_down.transpose(0, 2, 1)
-    wsend = jnp.stack(
-        [
-            jnp.concatenate(
-                [
-                    w_gate[:, :, i * FH : (i + 1) * FH],
-                    w_up[:, :, i * FH : (i + 1) * FH],
-                    down_t[:, :, i * FH : (i + 1) * FH],
-                    jnp.zeros((EXPERTS, SUB, FP - F3), BF16),
-                ],
-                axis=2,
-            )
-            for i in range(NXH)
-        ]
+    xin, info_all, w_all, wt = exchange(
+        activations, cotangent, slot_rows[0], slot_counts, route_probs[0], expert_ids,
+        w_gate, w_up, w_down,
     )
-
-    source = jnp.where(xl == 0, activations, cotangent).reshape(TOK, NZ, NY, SUB)
-    piece = lax.dynamic_index_in_dim(source, y, axis=2, keepdims=False).transpose(1, 2, 0)
-
-    position = jnp.arange(TOK, dtype=jnp.int32)
-    weight = jnp.where(position[None, :] < slot_counts[0][:, None], route_probs[0], 0.0)
-    hit = slot_rows[0][:, :, None] == position[None, None, :]
-    row_scale = jnp.sum(jnp.where(hit, weight[:, :, None], 0.0), axis=1)
-    info = jnp.concatenate(
-        [
-            row_scale,
-            jnp.broadcast_to(expert_ids[0].astype(F32)[:, None], (SLOTS, TOK)),
-            jnp.zeros((4, TOK), F32),
-        ]
-    )
-
-    xin, info_all, w_all, wt = exchange(piece, info, wsend)
     ids = info_all[:, :, 2:4, 0].astype(jnp.int32).reshape(-1)
     grad_gate, grad_up, grad_down, rows = layer(
         ids, xin, w_all.reshape(EXPERTS, DZ, FP), wt, info_all

time: 218 us -> 206 us (0.945); the launches traced: 215 us -> 206 us
  other arithmetic: 7.16 us -> 1.19 us
  local copies, waits for them, and re-layouts: 13.5 us -> 11.2 us
    another operation x2 -> x0, other arithmetic: 2.92 us -> none  [shards(): jnp.stack([jnp.concatenate([w_gate[:, :, i * FH:(i + 1) * FH], w_up[:, :,...]
    unnamed x23 -> x12, local copies, waits for them, and re-layouts: 10.6 us -> 10.6 us
where the time goes in v5:
time: 206 us
  Pallas kernels  193 us (94%)
  local copies, waits for them, and re-layouts  11.2 us (5%)
    pallas_call x1, Pallas kernels, layer(): pl.pallas_call(layer_kernel, out_shape=(jax.ShapeDtypeStruct((EXPERTS, SU...  156 us
    pallas_call x1, Pallas kernels, exchange(): pl.pallas_call(exchange_kernel, out_shape=(jax.ShapeDtypeStruct((NZ, DZ,...  36.6 us
    unnamed x12, local copies, waits for them, and re-layouts  10.6 us

profile of v5, /device:TPU:72, one launch (start us, length us, event | category | flops | bytes accessed | tf_op | source)
XLA Modules:
  0.0 205.8 jit_solution(17355506753414772053)
XLA Ops:
  0.6 0.0 copy-start.2
  0.6 2.3 %copy.18.wg = bf16[8,112,304]{2,1,0:T(8,128)(2,1)} copy(bf16[8,112,304]{1,2,0:T(8,128)(2,1)} %param.15) | data formatting | bytes 1089536 | tf_op args[6]
  2.9 0.0 copy-done.2
  2.9 1.1 copy.19.wu
  4.0 36.6 %exchange_in.1 = (bf16[8,448,128]{2,1,0:T(8,128)(2,1)}, f32[2,8,8,128]{3,2,1,0:T(8,128)}, bf16[8,4,112,464]{3,2,1,0:T(8,128)(2,1)}, bf16[8,464,448]{2,1,0:T(8,128)(2,1)}) custom-call(bf16[128,3584]{1,0:T(8,128)(2,1)} %act.1, bf16[128,3584]{1,0:T(8,128)(2,1)} %cot.1, s32[2,128]{1,0:T(2,128)} %bitcast.4, s32[1,2]{1,0:T(1,128)} %counts.1, f32[2,128]{1,0:T(2,128)} %bitcast.5, ...), custom_call_target="tpu_custom_call" | custom-call | tf_op jit(solution)/shard_map/exchange_in/pallas_call | solution.py:185
  40.6 1.2 convert_reduce_fusion
  41.8 0.6 convert_element_type.8.ids
  42.4 156.1 %layer.1 = (f32[8,112,304]{2,1,0:T(8,128)}, f32[8,112,304]{2,1,0:T(8,128)}, f32[8,304,112]{2,1,0:T(8,128)}, f32[128,448]{1,0:T(8,128)}) custom-call(s32[32]{0:T(128)} %convert_element_type.8.ids, bf16[8,448,128]{2,1,0:T(8,128)(2,1)} %get-tuple-element.13.xin, bf16[8,448,464]{2,1,0:T(8,128)(2,1)} %bitcast.3, bf16[8,464,448]{2,1,0:T(8,128)(2,1)} %get-tuple-element.15.wt, ...), custom_call_target="tpu_custom_call" | custom-call | tf_op jit(solution)/shard_map/layer/pallas_call | solution.py:644
  198.6 1.8 copy.20
  200.4 0.0 copy-start
  200.4 2.9 %copy.21 = f32[8,112,304]{1,2,0:T(8,128)} copy(f32[8,112,304]{2,1,0:T(8,128)} %get-tuple-element.25) | data formatting | bytes 2179072
  203.3 0.0 copy-done
  203.3 0.0 copy-start.1
  203.3 1.5 copy.22
  204.8 0.0 copy-done.1
  204.8 1.0 copy.24
Async XLA Ops:
  0.6 2.3 %copy-start.2 = (bf16[8,112,304]{1,2,0:T(8,128)(2,1)S(1)}, bf16[8,112,304]{1,2,0:T(8,128)(2,1)}, u32[]{:S(2)}) copy-start(bf16[8,112,304]{1,2,0:T(8,128)(2,1)} %param.16) | copy-start | bytes 1634308
  200.4 2.9 %copy-start = (f32[8,112,304]{2,1,0:T(8,128)S(1)}, f32[8,112,304]{2,1,0:T(8,128)}, u32[]{:S(2)}) copy-start(f32[8,112,304]{2,1,0:T(8,128)} %get-tuple-element.26) | copy-start | bytes 3268612
  203.3 1.5 copy-start.1

commit v6 on v5

--- a/solution.py
+++ b/solution.py
@@ -21,7 +21,7 @@
 NB = 3
 SWAP_AT = 7
 TURN_AT = 4
-VMEM_LIMIT = 58 * 1024 * 1024
+VMEM_LIMIT = 61 * 1024 * 1024
 
 
 def place():
@@ -64,22 +64,41 @@
     return [device(xl, y, (z + step) % NZ, xh, c) for step in range(1, NZ)]
 
 
-def exchange_kernel(
-    act, cot, rows, counts, probs, ids, wg, wu, wd, x_out, info_out, w_all, wt_out,
-    xt, stack, info, wsrc,
-    zs, zr, is_, ir, ys, yr, ixs, ixr, fs, fr, os_, or_, ps, pr, loc,
+def layer_kernel(
+    act, cot, rows_in, counts, probs, ids, wg, wu, wd, gate, up_out, down_out, xout,
+    xt, stack, info, numbers, wsrc, w, wt, xin, scale, experts,
+    x, early, first, acc, turn, own, dcat, hcat, dx, dxs, dw, wgot, wsnd, wfar,
+    a1, a2, b1, b2, sa, sb, done, mid, back,
+    zs, zr, is_, ir, js, jr, ys, yr, ixs, ixr, gs, gr, os_, or_, ps, pr, loc,
+    x_s, x_r, rs_s, rs_r, ag_s, ag_r,
+    a1s, a1r, b1s, b1r, a2s, a2r, b2s, b2r, ts, tr, fs, fr, ks, kr,
 ):
     xl, y, z, xh, c = me = place()
-    zp, yp = z_peers(*me), y_peers(*me)
+    ex = xl * NY + y
+    pos = xh * 2 + xl
+    hd = DZ // 2
+    zp, xp, yp = z_peers(*me), x_peers(*me), y_peers(*me)
+    up, down = zp[0], zp[NZ - 2]
+    to = (up, down)
     far = device(xl, y, z, 1 - xh, c)
     twin = device(xl, y, z, xh, 1 - c)
     part = pl.ds(pl.multiple_of(y * SUB, SUB), SUB)
     mine = 2 * xh + c
     other = 2 * (1 - xh) + c
+    pair = (ex + NZ - z) % NZ
+    along = device(xl, y, pair, xh, c)
+    across = device(pair // NY, pair % NY, z, xh, c)
+    before = (ex + z) % NZ
+    source = device(before // NY, before % NY, z, xh, c)
     barrier = pltpu.get_barrier_semaphore()
-    peers = zp + yp + [far, twin]
+    peers = zp + xp + yp + [twin]
     for dev in peers:
         pl.semaphore_signal(barrier, inc=1, device_id=dev, device_id_type=MESH)
+
+    @pl.when(z != 0)
+    def _():
+        pl.semaphore_signal(barrier, inc=1, device_id=across, device_id_type=MESH)
+        pl.semaphore_signal(barrier, inc=1, device_id=source, device_id_type=MESH)
 
     def pack(e, carry):
         g = wg[e].astype(F32)
@@ -91,19 +110,19 @@
             pieces.append(jnp.zeros((SUB, FP - F3), F32))
             both.append(jnp.concatenate(pieces, axis=1))
         wsrc[e] = jnp.where(xh == 0, both[1], both[0]).astype(BF16)
-        w_all[e, mine] = jnp.where(xh == 0, both[0], both[1]).astype(BF16)
+        w[e, mine] = jnp.where(xh == 0, both[0], both[1]).astype(BF16)
         return carry
 
     lax.fori_loop(0, EXPERTS, pack, 0)
-    pl.semaphore_wait(barrier, len(peers))
-
-    wfar = []
+    pl.semaphore_wait(barrier, len(peers) + jnp.where(z != 0, 2, 0))
+
+    wgone = []
     for e in range(EXPERTS):
-        wfar.append(remote(wsrc.at[e], w_all.at[e, mine], fs.at[e], fr.at[e], far))
-        wfar[-1].start()
+        wgone.append(remote(wsrc.at[e], w.at[e, mine], gs.at[e], gr.at[e], far))
+        wgone[-1].start()
     wown = []
     for e in range(EXPERTS):
-        wown.append(remote(w_all.at[e, mine], w_all.at[e, mine], os_.at[e], or_.at[e], twin))
+        wown.append(remote(w.at[e, mine], w.at[e, mine], os_.at[e], or_.at[e], twin))
         wown[-1].start()
 
     def turn_rows(j, carry):
@@ -118,33 +137,38 @@
 
     cz = []
     for i in range(NZ - 1):
-        to = (z + i + 1) % NZ
-        cz.append(remote(piece(to), x_out.at[z, part], zs.at[i], zr.at[i], zp[i]))
+        cz.append(remote(piece((z + i + 1) % NZ), xin.at[z, part], zs.at[i], zr.at[i], zp[i]))
         cz[-1].start()
 
     lane = lax.broadcasted_iota(jnp.int32, (1, TOK), 1)
     column = lax.broadcasted_iota(jnp.int32, (TOK, TOK), 1).astype(F32)
     for slot in range(SLOTS):
-        stack[slot : slot + 1, :] = rows[slot : slot + 1, :].astype(F32)
+        stack[slot : slot + 1, :] = rows_in[slot : slot + 1, :].astype(F32)
         stack[2 + slot : 3 + slot, :] = jnp.where(
             lane < counts[0, slot], probs[slot : slot + 1, :], 0.0
         )
     stack[4:8, :] = jnp.zeros((4, TOK), F32)
     turned = stack[...].T
     info[4:8, :] = jnp.zeros((4, TOK), F32)
+    numbers[...] = jnp.zeros((8, TOK), jnp.int32)
     for slot in range(SLOTS):
         hit = turned[:, slot : slot + 1] == column
         info[slot : slot + 1, :] = jnp.sum(
             jnp.where(hit, turned[:, 2 + slot : 3 + slot], 0.0), axis=0, keepdims=True
         )
-        info[2 + slot : 3 + slot, :] = jnp.full((1, TOK), ids[0, slot], jnp.int32).astype(F32)
+        number = jnp.full((1, TOK), ids[0, slot], jnp.int32)
+        numbers[slot : slot + 1, :] = number
+        info[2 + slot : 3 + slot, :] = number.astype(F32)
     ci = []
     for i in range(NZ - 1):
-        ci.append(remote(info, info_out.at[xh, z], is_.at[i], ir.at[i], zp[i]))
+        ci.append(remote(info, scale.at[xh, z], is_.at[i], ir.at[i], zp[i]))
+        ci[-1].start()
+        ci.append(remote(numbers, experts.at[xh, z], js.at[i], jr.at[i], zp[i]))
         ci[-1].start()
     here = [
-        pltpu.make_async_copy(piece(z), x_out.at[z, part], loc.at[0]),
-        pltpu.make_async_copy(info, info_out.at[xh, z], loc.at[1]),
+        pltpu.make_async_copy(piece(z), xin.at[z, part], loc.at[0]),
+        pltpu.make_async_copy(info, scale.at[xh, z], loc.at[1]),
+        pltpu.make_async_copy(numbers, experts.at[xh, z], loc.at[2]),
     ]
     for h in here:
         h.start()
@@ -154,94 +178,18 @@
         k.wait()
     cy = []
     for i in range(3):
-        cy.append(remote(x_out.at[:, part], x_out.at[:, part], ys.at[i], yr.at[i], yp[i]))
+        cy.append(remote(xin.at[:, part], xin.at[:, part], ys.at[i], yr.at[i], yp[i]))
         cy[-1].start()
     for k in ci:
         k.wait()
-    cinf = remote(info_out.at[xh], info_out.at[xh], ixs.at[0], ixr.at[0], far)
-    cinf.start()
-    wpass = []
-    for e in range(EXPERTS):
-        wfar[e].wait_recv()
-        wpass.append(
-            remote(w_all.at[e, other], w_all.at[e, other], ps.at[e], pr.at[e], twin)
-        )
-        wpass[-1].start()
-    for e in range(EXPERTS):
-        wown[e].wait_recv()
-        wpass[e].wait_recv()
-        wt_out[e] = w_all[e].reshape(DZ, FP).T
+    cinf = [
+        remote(scale.at[xh], scale.at[xh], ixs.at[0], ixr.at[0], far),
+        remote(experts.at[xh], experts.at[xh], ixs.at[1], ixr.at[1], far),
+    ]
+    for k in cinf:
+        k.start()
     for k in cy:
         k.wait()
-    cinf.wait()
-    for k in wfar + wown + wpass:
-        k.wait_send()
-
-
-def exchange(act, cot, rows, counts, probs, ids, wg, wu, wd):
-    dma = pltpu.SemaphoreType.DMA
-    vm = pl.BlockSpec(memory_space=pltpu.VMEM)
-    sm = pl.BlockSpec(memory_space=pltpu.SMEM)
-    return pl.pallas_call(
-        exchange_kernel,
-        out_shape=(
-            jax.ShapeDtypeStruct((NZ, DZ, TOK), BF16),
-            jax.ShapeDtypeStruct((NXH, NZ, 8, TOK), F32),
-            jax.ShapeDtypeStruct((EXPERTS, NXH * NC, SUB, FP), BF16),
-            jax.ShapeDtypeStruct((EXPERTS, FP, DZ), BF16),
-        ),
-        in_specs=[vm, vm, vm, sm, vm, sm, vm, vm, vm],
-        out_specs=(vm,) * 4,
-        scratch_shapes=[
-            pltpu.VMEM((NZ * DZ, TOK), BF16),
-            pltpu.VMEM((8, TOK), F32),
-            pltpu.VMEM((8, TOK), F32),
-            pltpu.VMEM((EXPERTS, SUB, FP), BF16),
-        ]
-        + [dma((7,))] * 4 + [dma((3,))] * 2 + [dma((1,))] * 2 + [dma((EXPERTS,))] * 6
-        + [dma((2,))],
-        compiler_params=pltpu.CompilerParams(
-            collective_id=0, has_side_effects=True, vmem_limit_bytes=VMEM_LIMIT
-        ),
-        name="exchange_in",
-    )(act, cot, rows, counts, probs, ids, wg, wu, wd)
-
-
-def layer_kernel(
-    ids, xin, w, wt, scale, gate, up_out, down_out, xout,
-    x, early, first, acc, turn, own, dcat, hcat, dx, dxs, dw, wgot, wsnd, wfar, a1, a2, b1, b2, sa, sb, done, mid, back,
-    x_s, x_r, rs_s, rs_r, ag_s, ag_r,
-    a1s, a1r, b1s, b1r, a2s, a2r, b2s, b2r, ts, tr, fs, fr, ks, kr,
-):
-    xl, y, z, xh, c = me = place()
-    ex = xl * NY + y
-    pos = xh * 2 + xl
-    hd = DZ // 2
-    xp, yp = x_peers(*me), y_peers(*me)
-    up = device(xl, y, (z + 1) % NZ, xh, c)
-    down = device(xl, y, (z + NZ - 1) % NZ, xh, c)
-    to = (up, down)
-    far = device(xl, y, z, 1 - xh, c)
-    twin = device(xl, y, z, xh, 1 - c)
-    pair = (ex + NZ - z) % NZ
-    along = device(xl, y, pair, xh, c)
-    across = device(pair // NY, pair % NY, z, xh, c)
-    before = (ex + z) % NZ
-    source = device(before // NY, before % NY, z, xh, c)
-    barrier = pltpu.get_barrier_semaphore()
-    for dev in xp + yp + [up, down, twin]:
-        pl.semaphore_signal(barrier, inc=1, device_id=dev, device_id_type=MESH)
-
-    @pl.when(pair != z)
-    def _():
-        pl.semaphore_signal(barrier, inc=1, device_id=along, device_id_type=MESH)
-
-    @pl.when(z != 0)
-    def _():
-        pl.semaphore_signal(barrier, inc=1, device_id=across, device_id_type=MESH)
-        pl.semaphore_signal(barrier, inc=1, device_id=source, device_id_type=MESH)
-
-    pl.semaphore_wait(barrier, 9 + jnp.where(pair != z, 1, 0) + jnp.where(z != 0, 2, 0))
 
     def lanes(half, gz):
         return pl.ds(pl.multiple_of((half * NZ + gz) * TOK, TOK), TOK)
@@ -264,16 +212,28 @@
         x[xl, :, lanes(xh, gz)] = xin[gz]
         for i in range(3):
             spread(s, i).wait_recv()
-
     spread_all(0)
     spread_all(1)
+    wpass = []
+    for e in range(EXPERTS):
+        wgone[e].wait_recv()
+        wpass.append(remote(w.at[e, other], w.at[e, other], ps.at[e], pr.at[e], twin))
+        wpass[-1].start()
+    for e in range(EXPERTS):
+        wown[e].wait_recv()
+        wpass[e].wait_recv()
+        wt[e] = w[e].reshape(DZ, FP).T
+    for k in cinf:
+        k.wait()
+    for k in wgone + wown + wpass:
+        k.wait_send()
 
     def partial(half, gz):
         at = lanes(half, gz)
         xt = x[0, :, at]
         dyt = x[1, :, at].astype(F32)
         for slot in range(SLOTS):
-            e = ids[half * (NZ * SLOTS) + gz * SLOTS + slot]
+            e = experts[half, gz, slot, 0]
             dys = (dyt * scale[half, gz, pl.ds(slot, 1), :]).astype(BF16)
             dcat[slot, :, at] = dys
             gu = jnp.dot(wt[e, 0 : 2 * FH, :], xt, preferred_element_type=F32)
@@ -367,10 +327,10 @@
     def rows(half, gz):
         total = jnp.zeros((DZ, TOK), F32)
         for slot in range(SLOTS):
-            e = ids[half * (NZ * SLOTS) + gz * SLOTS + slot]
+            e = experts[half, gz, slot, 0]
             hs = hcat[slot, 0 : 2 * FH, lanes(half, gz)]
             total = total + jnp.dot(
-                w[e, :, 0 : 2 * FH], hs, preferred_element_type=F32
+                w[e, :, :, 0 : 2 * FH].reshape(DZ, 2 * FH), hs, preferred_element_type=F32
             )
         q = spot(gz)
         dx[half, q // NY, q % NY] = total
@@ -635,9 +595,10 @@
     xout[...] = back[...].T
 
 
-def layer(ids, xin, w, wt, scale):
+def layer(act, cot, rows, counts, probs, ids, wg, wu, wd):
     dma = pltpu.SemaphoreType.DMA
     vm = pl.BlockSpec(memory_space=pltpu.VMEM)
+    sm = pl.BlockSpec(memory_space=pltpu.SMEM)
     hd = DZ // 2
     cols = NXH * NZ * TOK
     block = (EXPERTS, SUB, FP)
@@ -649,9 +610,19 @@
             jax.ShapeDtypeStruct((EXPERTS, 2 * FH, SUB), F32),
             jax.ShapeDtypeStruct((TOK, DZ), F32),
         ),
-        in_specs=[pl.BlockSpec(memory_space=pltpu.SMEM), vm, vm, vm, vm],
+        in_specs=[vm, vm, vm, sm, vm, sm, vm, vm, vm],
         out_specs=(vm,) * 4,
         scratch_shapes=[
+            pltpu.VMEM((NZ * DZ, TOK), BF16),
+            pltpu.VMEM((8, TOK), F32),
+            pltpu.VMEM((8, TOK), F32),
+            pltpu.VMEM((8, TOK), jnp.int32),
+            pltpu.VMEM(block, BF16),
+            pltpu.VMEM((EXPERTS, NXH * NC, SUB, FP), BF16),
+            pltpu.VMEM((EXPERTS, FP, DZ), BF16),
+            pltpu.VMEM((NZ, DZ, TOK), BF16),
+            pltpu.VMEM((NXH, NZ, 8, TOK), F32),
+            pltpu.VMEM((NXH, NZ, 8, TOK), jnp.int32),
             pltpu.VMEM((2, DZ, cols), BF16),
             pltpu.VMEM((2, NB, SLOTS, FP, TOK), BF16),
             pltpu.VMEM((2, SLOTS, FP, TOK), BF16),
@@ -675,9 +646,10 @@
             pltpu.VMEM((DZ, TOK), F32),
             pltpu.VMEM((DZ, TOK), F32),
             pltpu.VMEM((DZ, TOK), F32),
-            dma((NZ, 3)),
-            dma((NZ, 3)),
         ]
+        + [dma((NZ - 1,))] * 6 + [dma((3,))] * 2 + [dma((2,))] * 2 + [dma((EXPERTS,))] * 6
+        + [dma((3,))]
+        + [dma((NZ, 3))] * 2
         + [dma((2, NZ - 1, SLOTS))] * 4
         + [dma((2, NZ)), dma((3, NXH, NXL)), dma((2, NZ)), dma((3, NY))]
         + [dma((3,))] * 4
@@ -685,22 +657,18 @@
         + [dma((EXPERTS,))] * 2
         + [dma((2,))] * 2,
         compiler_params=pltpu.CompilerParams(
-            collective_id=1, has_side_effects=True, vmem_limit_bytes=VMEM_LIMIT
+            collective_id=0, has_side_effects=True, vmem_limit_bytes=VMEM_LIMIT
         ),
         name="layer",
-    )(ids, xin, w, wt, scale)
+    )(act, cot, rows, counts, probs, ids, wg, wu, wd)
 
 
 def shards(
     activations, cotangent, expert_ids, slot_rows, slot_counts, route_probs, w_gate, w_up, w_down
 ):
-    xin, info_all, w_all, wt = exchange(
+    grad_gate, grad_up, grad_down, rows = layer(
         activations, cotangent, slot_rows[0], slot_counts, route_probs[0], expert_ids,
         w_gate, w_up, w_down,
-    )
-    ids = info_all[:, :, 2:4, 0].astype(jnp.int32).reshape(-1)
-    grad_gate, grad_up, grad_down, rows = layer(
-        ids, xin, w_all.reshape(EXPERTS, DZ, FP), wt, info_all
     )
     return rows, grad_gate, grad_up, grad_down
 

time: 206 us -> 192 us (0.932)
  Pallas kernels: 193 us -> 181 us
    pallas_call x1 -> x0, Pallas kernels: 36.6 us -> none  [exchange(): pl.pallas_call(exchange_kernel, out_shape=(jax.ShapeDtypeStruct((NZ, DZ,...]
    pallas_call x1, Pallas kernels: 156 us -> 181 us  [layer(): pl.pallas_call(layer_kernel, out_shape=(jax.ShapeDtypeStruct((EXPERTS, SU...]
where the time goes in v6:
time: 192 us
  Pallas kernels  181 us (94%)
  local copies, waits for them, and re-layouts  10.6 us (6%)
    pallas_call x1, Pallas kernels, layer(): pl.pallas_call(layer_kernel, out_shape=(jax.ShapeDtypeStruct((EXPERTS, SU...  181 us
    unnamed x12, local copies, waits for them, and re-layouts  10.6 us

profile of v6, /device:TPU:72, one launch (start us, length us, event | category | flops | bytes accessed | tf_op | source)
XLA Modules:
  0.0 192.2 jit_solution(11239244647356701231)
XLA Ops:
  0.6 0.0 copy-start.2
  0.6 2.3 %copy.13.wg = bf16[8,112,304]{2,1,0:T(8,128)(2,1)} copy(bf16[8,112,304]{1,2,0:T(8,128)(2,1)} %param.15) | data formatting | bytes 1089536 | tf_op args[6]
  2.9 0.0 copy-done.2
  2.9 1.1 copy.14.wu
  4.0 180.9 %layer.1 = (f32[8,112,304]{2,1,0:T(8,128)}, f32[8,112,304]{2,1,0:T(8,128)}, f32[8,304,112]{2,1,0:T(8,128)}, f32[128,448]{1,0:T(8,128)}) custom-call(bf16[128,3584]{1,0:T(8,128)(2,1)} %act.1, bf16[128,3584]{1,0:T(8,128)(2,1)} %cot.1, s32[2,128]{1,0:T(2,128)} %bitcast.2, s32[1,2]{1,0:T(1,128)} %counts.1, f32[2,128]{1,0:T(2,128)} %bitcast.3, s32[1,2]{1,0:T(1,128)} %ids.1, ...), custom_call_target="tpu_custom_call" | custom-call | tf_op jit(solution)/shard_map/layer/pallas_call | solution.py:605
  184.9 1.8 copy.15
  186.7 0.0 copy-start
  186.7 2.9 %copy.16 = f32[8,112,304]{1,2,0:T(8,128)} copy(f32[8,112,304]{2,1,0:T(8,128)} %get-tuple-element.13) | data formatting | bytes 2179072
  189.7 0.0 copy-done
  189.7 0.0 copy-start.1
  189.7 1.5 copy.17
  191.2 0.0 copy-done.1
  191.2 1.0 copy.19
Async XLA Ops:
  0.6 2.3 %copy-start.2 = (bf16[8,112,304]{1,2,0:T(8,128)(2,1)S(1)}, bf16[8,112,304]{1,2,0:T(8,128)(2,1)}, u32[]{:S(2)}) copy-start(bf16[8,112,304]{1,2,0:T(8,128)(2,1)} %param.16) | copy-start | bytes 1634308
  186.7 2.9 %copy-start = (f32[8,112,304]{2,1,0:T(8,128)S(1)}, f32[8,112,304]{2,1,0:T(8,128)}, u32[]{:S(2)}) copy-start(f32[8,112,304]{2,1,0:T(8,128)} %get-tuple-element.14) | copy-start | bytes 3268612
  189.7 1.5 copy-start.1

commit v7 on v6

--- a/solution.py
+++ b/solution.py
@@ -65,10 +65,10 @@
 
 
 def layer_kernel(
-    act, cot, rows_in, counts, probs, ids, wg, wu, wd, gate, up_out, down_out, xout,
+    act, cot, rows_in, counts, probs, ids, wg, wu, wd, gate, up_out, down_out, back,
     xt, stack, info, numbers, wsrc, w, wt, xin, scale, experts,
     x, early, first, acc, turn, own, dcat, hcat, dx, dxs, dw, wgot, wsnd, wfar,
-    a1, a2, b1, b2, sa, sb, done, mid, back,
+    a1, a2, b1, b2, sa, sb, done, mid,
     zs, zr, is_, ir, js, jr, ys, yr, ixs, ixr, gs, gr, os_, or_, ps, pr, loc,
     x_s, x_r, rs_s, rs_r, ag_s, ag_r,
     a1s, a1r, b1s, b1r, a2s, a2r, b2s, b2r, ts, tr, fs, fr, ks, kr,
@@ -103,14 +103,14 @@
     def pack(e, carry):
         g = wg[e].astype(F32)
         u = wu[e].astype(F32)
-        d = wd[e].astype(F32).T
+        d = wd[e].astype(F32)
         both = []
         for i in range(NXH):
-            pieces = [v[:, i * FH : (i + 1) * FH] for v in (g, u, d)]
-            pieces.append(jnp.zeros((SUB, FP - F3), F32))
-            both.append(jnp.concatenate(pieces, axis=1))
-        wsrc[e] = jnp.where(xh == 0, both[1], both[0]).astype(BF16)
-        w[e, mine] = jnp.where(xh == 0, both[0], both[1]).astype(BF16)
+            pieces = [v[i * FH : (i + 1) * FH] for v in (g, u, d)]
+            pieces.append(jnp.zeros((FP - F3, SUB), F32))
+            both.append(jnp.concatenate(pieces, axis=0))
+        wsrc[e] = jnp.where(xh == 0, both[1], both[0]).T.astype(BF16)
+        w[e, mine] = jnp.where(xh == 0, both[0], both[1]).T.astype(BF16)
         return carry
 
     lax.fori_loop(0, EXPERTS, pack, 0)
@@ -506,11 +506,11 @@
         away(e).wait_recv()
         ours = wgot[1, e]
         theirs = wfar[e].astype(F32)
-        low = jnp.where(xh == 0, ours, theirs)
-        high = jnp.where(xh == 0, theirs, ours)
-        gate[e] = jnp.concatenate([low[:, 0:FH], high[:, 0:FH]], axis=1)
-        up_out[e] = jnp.concatenate([low[:, FH : 2 * FH], high[:, FH : 2 * FH]], axis=1)
-        down_out[e] = jnp.concatenate([low[:, 2 * FH : F3].T, high[:, 2 * FH : F3].T], axis=0)
+        low = jnp.where(xh == 0, ours, theirs).T
+        high = jnp.where(xh == 0, theirs, ours).T
+        for i, out in enumerate((gate, up_out, down_out)):
+            out[e, 0:FH, :] = low[i * FH : (i + 1) * FH]
+            out[e, FH : 2 * FH, :] = high[i * FH : (i + 1) * FH]
 
     def per_expert(e, carry):
         weights(e)
@@ -591,8 +591,6 @@
     @pl.when(z != 0)
     def _():
         second_step().wait()
-
-    xout[...] = back[...].T
 
 
 def layer(act, cot, rows, counts, probs, ids, wg, wu, wd):
@@ -605,10 +603,10 @@
     return pl.pallas_call(
         layer_kernel,
         out_shape=(
-            jax.ShapeDtypeStruct((EXPERTS, SUB, 2 * FH), F32),
-            jax.ShapeDtypeStruct((EXPERTS, SUB, 2 * FH), F32),
             jax.ShapeDtypeStruct((EXPERTS, 2 * FH, SUB), F32),
-            jax.ShapeDtypeStruct((TOK, DZ), F32),
+            jax.ShapeDtypeStruct((EXPERTS, 2 * FH, SUB), F32),
+            jax.ShapeDtypeStruct((EXPERTS, 2 * FH, SUB), F32),
+            jax.ShapeDtypeStruct((DZ, TOK), F32),
         ),
         in_specs=[vm, vm, vm, sm, vm, sm, vm, vm, vm],
         out_specs=(vm,) * 4,
@@ -645,7 +643,6 @@
             pltpu.VMEM((NY, hd, TOK), F32),
             pltpu.VMEM((DZ, TOK), F32),
             pltpu.VMEM((DZ, TOK), F32),
-            pltpu.VMEM((DZ, TOK), F32),
         ]
         + [dma((NZ - 1,))] * 6 + [dma((3,))] * 2 + [dma((2,))] * 2 + [dma((EXPERTS,))] * 6
         + [dma((3,))]
@@ -668,9 +665,9 @@
 ):
     grad_gate, grad_up, grad_down, rows = layer(
         activations, cotangent, slot_rows[0], slot_counts, route_probs[0], expert_ids,
-        w_gate, w_up, w_down,
+        w_gate.transpose(0, 2, 1), w_up.transpose(0, 2, 1), w_down,
     )
-    return rows, grad_gate, grad_up, grad_down
+    return rows.T, grad_gate.transpose(0, 2, 1), grad_up.transpose(0, 2, 1), grad_down
 
 
 def solution(mesh):

time: 192 us -> 188 us (0.979)
  the two profiles are of different devices: /device:TPU:72 before, /device:TPU:32 now
where the time goes in v7:
time: 188 us
  Pallas kernels  180 us (96%)
  local copies, waits for them, and re-layouts  6.93 us (4%)
    pallas_call x1, Pallas kernels, layer(): pl.pallas_call(layer_kernel, out_shape=(jax.ShapeDtypeStruct((EXPERTS, 2...  180 us
    unnamed x8, local copies, waits for them, and re-layouts  6.93 us

profile of v7, /device:TPU:32, one launch (start us, length us, event | category | flops | bytes accessed | tf_op | source)
XLA Modules:
  0.0 187.8 jit_solution(7377933768631545226)
XLA Ops:
  0.6 180.2 %layer.1 = (f32[8,304,112]{2,1,0:T(8,128)}, f32[8,304,112]{2,1,0:T(8,128)}, f32[8,304,112]{2,1,0:T(8,128)}, f32[448,128]{1,0:T(8,128)}) custom-call(bf16[128,3584]{1,0:T(8,128)(2,1)} %act.1, bf16[128,3584]{1,0:T(8,128)(2,1)} %cot.1, s32[2,128]{1,0:T(2,128)} %bitcast.12, s32[1,2]{1,0:T(1,128)} %counts.1, f32[2,128]{1,0:T(2,128)} %bitcast.13, s32[1,2]{1,0:T(1,128)} %ids.1, ...), custom_call_target="tpu_custom_call" | custom-call | tf_op jit(solution)/shard_map/layer/pallas_call | solution.py:603
  180.9 1.6 copy.17
  182.5 0.0 copy-start.1
  182.5 2.5 %copy.18 = f32[8,112,304]{1,2,0:T(8,128)} copy(f32[8,112,304]{1,2,0:T(8,128)} %bitcast.8) | data formatting | bytes 2179072
  185.0 0.0 copy-done.1
  185.0 0.0 copy-start
  185.0 1.0 copy.19
  186.1 0.7 copy-done
  186.8 1.0 copy.20
Async XLA Ops:
  182.5 2.5 %copy-start.1 = (f32[8,304,112]{2,1,0:T(8,128)S(1)}, f32[8,304,112]{2,1,0:T(8,128)}, u32[]{:S(2)}) copy-start(f32[8,304,112]{2,1,0:T(8,128)} %get-tuple-element.10) | copy-start | bytes 3268612
  185.0 1.7 copy-start

commit v8 on v7

--- a/solution.py
+++ b/solution.py
@@ -18,7 +18,7 @@
 FH = 152
 F3 = 3 * FH
 FP = 464
-NB = 3
+NB = 4
 SWAP_AT = 7
 TURN_AT = 4
 VMEM_LIMIT = 61 * 1024 * 1024

time: 188 us -> 183 us (0.973)
  the two profiles are of different devices: /device:TPU:32 before, /device:TPU:72 now
where the time goes in v8:
time: 183 us; the launch traced here: 180 us
  Pallas kernels  172 us (94%)
  local copies, waits for them, and re-layouts  6.93 us (4%)
    pallas_call x1, Pallas kernels, layer(): pl.pallas_call(layer_kernel, out_shape=(jax.ShapeDtypeStruct((EXPERTS, 2...  172 us
    unnamed x8, local copies, waits for them, and re-layouts  6.93 us

profile of v8, /device:TPU:72, one launch (start us, length us, event | category | flops | bytes accessed | tf_op | source)
XLA Modules:
  0.0 179.8 jit_solution(16285367912893961652)
XLA Ops:
  0.6 172.2 %layer.1 = (f32[8,304,112]{2,1,0:T(8,128)}, f32[8,304,112]{2,1,0:T(8,128)}, f32[8,304,112]{2,1,0:T(8,128)}, f32[448,128]{1,0:T(8,128)}) custom-call(bf16[128,3584]{1,0:T(8,128)(2,1)} %act.1, bf16[128,3584]{1,0:T(8,128)(2,1)} %cot.1, s32[2,128]{1,0:T(2,128)} %bitcast.12, s32[1,2]{1,0:T(1,128)} %counts.1, f32[2,128]{1,0:T(2,128)} %bitcast.13, s32[1,2]{1,0:T(1,128)} %ids.1, ...), custom_call_target="tpu_custom_call" | custom-call | tf_op jit(solution)/shard_map/layer/pallas_call | solution.py:603
  172.9 1.6 copy.17
  174.5 0.0 copy-start.1
  174.5 2.5 %copy.18 = f32[8,112,304]{1,2,0:T(8,128)} copy(f32[8,112,304]{1,2,0:T(8,128)} %bitcast.8) | data formatting | bytes 2179072
  177.0 0.0 copy-done.1
  177.0 0.0 copy-start
  177.0 1.0 copy.19
  178.1 0.7 copy-done
  178.8 1.0 copy.20
Async XLA Ops:
  174.5 2.5 %copy-start.1 = (f32[8,304,112]{2,1,0:T(8,128)S(1)}, f32[8,304,112]{2,1,0:T(8,128)}, u32[]{:S(2)}) copy-start(f32[8,304,112]{2,1,0:T(8,128)} %get-tuple-element.10) | copy-start | bytes 3268612
  177.0 1.7 copy-start
